TPU v7x, 128 devices: a whole 4x4x4 slice. The times are simulated.
128 devices in a mesh: ctx: 16 (over x, y), tp: 8 (over z, core).
Axes of the slice: x: 4, y: 4, z: 4, core: 2. Of those that a mesh axis runs over, the one named last changes fastest.
Arguments:
- rotated_queries: bfloat16 [8192, 8192], P('ctx', 'tp'), may hold values from -25 to 25
- rotated_keys: bfloat16 [8192, 1024], P('ctx', 'tp'), may hold values from -25 to 25
- value_matrix: bfloat16 [8192, 1024], P('ctx', 'tp'), may hold values from -6 to 6
- out_weight: bfloat16 [8192, 8192], P('tp', 'ctx'), may hold values from -0.0625 to 0.0625
- doc_ids: int32 [8192], replicated, may hold values from 0 to 7, never falling along the last dimension, each value on 1 to 2048 neighbouring positions
- assignment: int32 [16, 16], replicated, may hold values from 0 to 15, each once within a row
Outputs:
- owner_output: bfloat16 [8192, 8192], P('ctx', 'tp')
Inputs may be any that keep to these rules, and one draw needn't show every extreme that they name: Each row of assignment is a permutation of 0 to 15. `doc_ids`: documents are numbered in order along the tokens; each has 1 to 2048 tokens and one has exactly 2048.
All inputs are finite; a program needn't handle non-finite values.
Results may differ from a plain program's by a relative error of at most 0.017.
Values may be sent and summed in bfloat16 or wider, within the bound.
No kernel may reach another device: no remote copies, remote signals or barrier semaphores. Data moves between devices by JAX's collectives and lax.ppermute only.
A program may use at most 320 MiB of HBM per device.

v0:
```python
import functools
import math

import jax
import jax.numpy as jnp
from jax import lax
from jax.experimental import pallas as pl
from jax.experimental.pallas import tpu as pltpu
from jax.sharding import PartitionSpec as P

HEAD_WIDTH = 128
NDOC = 8
SIDE = 4
SCALE = math.log2(math.e) / math.sqrt(HEAD_WIDTH)
TILE = 256
GROUP = 4


def grid_shift(dx, dy):
    return [
        (4 * x + y, 4 * ((x + dx) % 4) + (y + dy) % 4) for x in range(4) for y in range(4)
    ]


def z_shift(steps):
    return [(t, (t + 2 * steps) % 8) for t in range(8)]


CORES = [(t, t ^ 1) for t in range(8)]


def attend_kernel(firsts_ref, q_ref, *rest):
    parts = rest[:5]
    outs, (window, stacked, top, total, acc) = rest[5:-5], rest[-5:]
    step = pl.program_id(0)
    span = parts[0].shape[0]
    tokens = q_ref.shape[0]
    heads = q_ref.shape[1] // HEAD_WIDTH

    @pl.when(step == 0)
    def _():
        for k in range(5):
            window[pl.ds(k * span, span), :] = parts[k][...]

    for h in range(heads):
        stacked[pl.ds(h * tokens, tokens), :] = q_ref[:, h * HEAD_WIDTH : (h + 1) * HEAD_WIDTH]
    first = 4 * span + step * tokens

    def beginning(position):
        at = firsts_ref[0]
        for d in range(1, NDOC):
            at = jnp.where(position >= firsts_ref[d], firsts_ref[d], at)
        return at

    low = beginning(first) // tokens
    full = first // tokens
    plain = jnp.clip((beginning(first + tokens - 1) + tokens - 1) // tokens, low, full)
    begins = beginning(first + lax.broadcasted_iota(jnp.int32, (tokens, 1), 0))
    top[...] = jnp.full_like(top, -1e30)
    total[...] = jnp.zeros_like(total)
    acc[...] = jnp.zeros_like(acc)

    def absorb(start, size, masked):
        place = pl.ds(pl.multiple_of(start, tokens), size)
        keys, values = window[place, :HEAD_WIDTH], window[place, HEAD_WIDTH:]
        if masked:
            there = lax.broadcasted_iota(jnp.int32, (tokens, size), 1) + start
            here = lax.broadcasted_iota(jnp.int32, (tokens, size), 0) + first
            seen = (there >= begins) & (there <= here)
        for g in range(heads // GROUP):
            rows = slice(g * GROUP * tokens, (g + 1) * GROUP * tokens)
            s = lax.dot_general(
                stacked[rows], keys, (((1,), (1,)), ((), ())), preferred_element_type=jnp.float32
            )
            if masked:
                s = jnp.where(seen[None], s.reshape(GROUP, tokens, size), -1e30)
                s = s.reshape(GROUP * tokens, size)
            old = top[rows]
            new = jnp.maximum(old, jnp.max(s, axis=1, keepdims=True))
            peak = jnp.maximum(new, -1e29)
            fade = jnp.exp2((old - peak) * SCALE)
            run, pieces = total[rows] * fade, []
            for k in range(size // 128):
                e = jnp.exp2((s[:, k * 128 : (k + 1) * 128] - peak) * SCALE)
                run = run + e
                pieces.append(e.astype(jnp.bfloat16))
            top[rows] = new
            total[rows] = run
            acc[rows] = acc[rows] * fade + jnp.dot(
                jnp.concatenate(pieces, axis=1), values, preferred_element_type=jnp.float32
            )

    def sweep(begin, end, masked):
        pairs = (end - begin) // 2
        lax.fori_loop(
            0, pairs, lambda i, _: absorb((begin + 2 * i) * tokens, 2 * tokens, masked), None
        )

        @pl.when((end - begin) % 2 == 1)
        def _():
            absorb((end - 1) * tokens, tokens, masked)

    sweep(low, plain, True)
    sweep(plain, full, False)
    absorb(first, tokens, True)
    result = acc[...] / jnp.sum(total[...], axis=1, keepdims=True)
    for k in range(len(outs)):

        @pl.when(step == k)
        def _():
            for h in range(heads):
                outs[k][:, h * HEAD_WIDTH : (h + 1) * HEAD_WIDTH] = result[
                    h * tokens : (h + 1) * tokens
                ].astype(outs[k].dtype)


def attend(queries, parts, firsts):
    tokens, width = queries.shape
    span = parts[0].shape[0]
    rows = TILE * width // HEAD_WIDTH
    return pl.pallas_call(
        attend_kernel,
        grid_spec=pltpu.PrefetchScalarGridSpec(
            num_scalar_prefetch=1,
            grid=(tokens // TILE,),
            in_specs=[
                pl.BlockSpec((TILE, width), lambda i, b: (i, 0)),
            ]
            + [pl.BlockSpec((span, 2 * HEAD_WIDTH), lambda i, b: (0, 0))] * 5,
            out_specs=[pl.BlockSpec((TILE, width), lambda i, b: (0, 0))] * (tokens // TILE),
            scratch_shapes=[
                pltpu.VMEM((5 * span, 2 * HEAD_WIDTH), jnp.bfloat16),
                pltpu.VMEM((rows, HEAD_WIDTH), jnp.bfloat16),
                pltpu.VMEM((rows, 128), jnp.float32),
                pltpu.VMEM((rows, 128), jnp.float32),
                pltpu.VMEM((rows, 128), jnp.float32),
            ],
        ),
        out_shape=[jax.ShapeDtypeStruct((TILE, width), jnp.bfloat16)] * (tokens // TILE),
        compiler_params=pltpu.CompilerParams(vmem_limit_bytes=24 * 1024 * 1024),
        cost_estimate=pl.CostEstimate(
            flops=1, bytes_accessed=1, transcendentals=0
        ),
    )(firsts, queries, *parts)


def document_starts(doc_ids, me, tokens):
    docs = jnp.arange(NDOC, dtype=jnp.int32)
    first = jnp.sum((doc_ids[None, :] < docs[:, None]).astype(jnp.int32), axis=1)
    return first - (me - 4) * tokens


def project_kernel(count, turn_ref, *refs):
    mine, partner = refs[:count], refs[count : 2 * count]
    weights, rest = refs[2 * count : 2 * count + 2 * SIDE], refs[2 * count + 2 * SIDE :]
    *arrays, held = rest
    if len(arrays) > SIDE:
        arrays[-1][...] = sum_of(arrays[:SIDE])
        arrays = arrays[SIDE:-1]
    for d in range(SIDE):
        row = 0
        for a, b in zip(mine, partner):
            r = jnp.dot(a[...], weights[2 * d][...], preferred_element_type=jnp.float32)
            r += jnp.dot(b[...], weights[2 * d + 1][...], preferred_element_type=jnp.float32)
            held[d, row : row + a.shape[0]] = r.astype(held.dtype)
            row += a.shape[0]
    for e in range(SIDE):
        arrays[e][...] = held[lax.rem(turn_ref[0] + e, SIDE)]


def sum_of(terms):
    r = terms[0][...].astype(jnp.float32)
    for t in terms[1:]:
        r += t[...].astype(jnp.float32)
    return r.astype(terms[0].dtype)


def project(turn, mine, partner, weights, finished):
    count = len(mine)
    rows = sum(a.shape[0] for a in mine)
    out = jax.ShapeDtypeStruct((rows, weights[0].shape[1]), jnp.bfloat16)
    vmem = pl.BlockSpec(memory_space=pltpu.VMEM)
    number = SIDE + (1 if finished else 0)
    outs = pl.pallas_call(
        functools.partial(project_kernel, count),
        in_specs=[pl.BlockSpec(memory_space=pltpu.SMEM)]
        + [vmem] * (2 * count + 2 * SIDE + len(finished)),
        out_specs=[vmem] * number,
        out_shape=[out] * number,
        scratch_shapes=[pltpu.VMEM((SIDE,) + out.shape, out.dtype)],
        compiler_params=pltpu.CompilerParams(vmem_limit_bytes=10 * 1024 * 1024),
        cost_estimate=pl.CostEstimate(flops=1, bytes_accessed=1, transcendentals=0),
    )(turn, *mine, *partner, *weights, *finished)
    return outs[:SIDE], outs[SIDE:]


def after(value, *others):
    return lax.optimization_barrier((value,) + others)[0]


def meet(*groups):
    flat = lax.optimization_barrier(tuple(a for g in groups for a in g))
    out, at = [], 0
    for g in groups:
        out.append(list(flat[at : at + len(g)]))
        at += len(g)
    return out


def spread_z(pieces):
    return [pieces[0]] + [lax.ppermute(pieces[e], "tp", z_shift(e)) for e in range(1, SIDE)]


def collect_kernel(y_ref, sources_ref, *refs):
    *terms, out_ref, held = refs
    groups = [terms[:1], terms[1:2], terms[2 : 2 + SIDE], terms[2 + SIDE :]]
    block = out_ref.shape[2]
    half = terms[0].shape[0] // 2
    places = (((0, 0), (0, 8)), ((1, 0), (3, 8)), ((1, 8), (3, 0)), ((2, 0), (2, 8)))
    for group, pair in zip(groups, places):
        r = sum_of(group)
        for k, (d, first) in enumerate(pair):
            for b in range(half // block):
                row = k * half + b * block
                held[d, first + b] = r[row : row + block]
    for source in range(SIDE):
        d = lax.rem(source - y_ref[0] + SIDE, SIDE)
        for o in range(out_ref.shape[0]):
            out_ref[o, source] = held[d, sources_ref[source, o]]


def collect(y, sources, own, outer, inner, far):
    terms = [*own, *outer, *inner, *far]
    rows, part = terms[0].shape
    owners = sources.shape[1]
    block = rows // owners
    smem = pl.BlockSpec(memory_space=pltpu.SMEM)
    shape = (owners, SIDE, block, part)
    return pl.pallas_call(
        collect_kernel,
        grid=(1,),
        in_specs=[smem] * 2 + [pl.BlockSpec((rows, part), lambda i: (0, 0))] * len(terms),
        out_specs=pl.BlockSpec(shape, lambda i: (0, 0, 0, 0)),
        out_shape=jax.ShapeDtypeStruct(shape, jnp.bfloat16),
        scratch_shapes=[pltpu.VMEM((SIDE, owners, block, part), jnp.bfloat16)],
        compiler_params=pltpu.CompilerParams(vmem_limit_bytes=16 * 1024 * 1024),
        cost_estimate=pl.CostEstimate(flops=1, bytes_accessed=1, transcendentals=0),
    )(y, sources, *terms)


def assemble_kernel(core_ref, here_ref, swapped_ref, out_ref):
    block, part = here_ref.shape[-2:]
    for core in range(2):

        @pl.when(core_ref[0] == core)
        def _():
            for x in range(SIDE):
                for source in range(SIDE):
                    row = (x * SIDE + source) * block
                    for p in range(2):
                        stay = here_ref[x, core, p, source]
                        came = swapped_ref[x, p, source]
                        for c, piece in ((core, stay), (1 - core, came)):
                            col = (2 * p + c) * part
                            out_ref[row : row + block, col : col + part] = piece


def assemble(core, here, swapped):
    block, part = here.shape[-2:]
    vmem = pl.BlockSpec(memory_space=pltpu.VMEM)
    return pl.pallas_call(
        assemble_kernel,
        in_specs=[pl.BlockSpec(memory_space=pltpu.SMEM)] + [vmem] * 2,
        out_specs=vmem,
        out_shape=jax.ShapeDtypeStruct((SIDE * SIDE * block, 4 * part), jnp.bfloat16),
        compiler_params=pltpu.CompilerParams(vmem_limit_bytes=8 * 1024 * 1024),
        cost_estimate=pl.CostEstimate(flops=1, bytes_accessed=1, transcendentals=0),
    )(core, here, swapped)


def shards(rotated_queries, rotated_keys, value_matrix, out_weight, doc_ids, assignment):
    me, lane = lax.axis_index("ctx"), lax.axis_index("tp")
    x, y = me // SIDE, me % SIDE
    z, core = lane // 2, lane % 2
    tokens = rotated_queries.shape[0]
    owners = lax.axis_size("ctx")
    block = tokens // owners
    part = out_weight.shape[1] // 2

    both = jnp.concatenate([rotated_keys, value_matrix], axis=1)
    above = lax.ppermute(both, "ctx", grid_shift(1, 0))
    near = [
        lax.ppermute(jnp.where(y + k < SIDE, both, above), "ctx", grid_shift(0, k))
        for k in range(1, SIDE)
    ]
    firsts = document_starts(doc_ids, me, tokens)

    kept = lax.dynamic_slice_in_dim(out_weight, core * part, part, axis=1)
    given = lax.dynamic_slice_in_dim(out_weight, (1 - core) * part, part, axis=1)
    taken = lax.ppermute(given, "tp", CORES)
    kept_next, taken_next = [lax.ppermute(a, "ctx", grid_shift(-1, 0)) for a in (kept, taken)]
    taken_last, kept_last = [lax.ppermute(a, "ctx", grid_shift(1, 0)) for a in (taken, kept)]
    near, (kept_next, taken_last) = meet(near, [kept_next, taken_last])
    kept_far = lax.ppermute(kept_next, "ctx", grid_shift(-1, 0))
    taken_far = lax.ppermute(taken_last, "ctx", grid_shift(1, 0))
    weights = [kept, taken, kept_next, taken_next, kept_far, taken_far, kept_last, taken_last]
    turn = ((z - x) % SIDE).reshape(1)
    window = [above] + near[::-1] + [both]

    def swap(a):
        return lax.ppermute(a, "tp", CORES)

    def along(a, steps):
        return lax.ppermute(a, "ctx", grid_shift(0, -steps))

    def terms(mine, partner=None, finished=()):
        partner = partner or [swap(a) for a in mine]
        pieces, total = project(turn, mine, partner, weights, finished)
        return spread_z(pieces), total

    head, tail = attend(rotated_queries, window, firsts)
    (head, tail), weights = meet([head, tail], weights)
    swaps = [swap(head), swap(tail)]
    outer = [along(head, 1), along(tail, 3)]
    own, _ = terms([head, tail], swaps)
    outer, pair, _ = meet(outer, [tail, head], own[:1])
    inner = [along(pair[0], 1), along(pair[1], 3)]
    outer_terms, _ = terms(outer)
    inner, outer, own, _ = meet(inner, outer, own, outer_terms[:1])
    far = [along(outer[0], 1), along(outer[1], 3)]
    inner_terms, own = terms(inner, finished=own)
    far, outer_terms, _ = meet(far, outer_terms, inner_terms[:1])
    far_terms, outer = terms(far, finished=outer_terms)
    inner_terms, far_terms = meet(inner_terms, far_terms)
    sources = lax.dynamic_slice_in_dim(assignment, x * SIDE, SIDE, axis=0)
    outgoing = collect(y.reshape(1), sources, own, outer, inner_terms, far_terms)
    arrived = lax.all_to_all(outgoing, "ctx", split_axis=0, concat_axis=0, tiled=True)
    arrived = arrived.reshape(SIDE, 2, 2, SIDE, block, part)
    leave = lax.dynamic_index_in_dim(arrived, 1 - core, 1, keepdims=False)
    return assemble(core.reshape(1), arrived, swap(leave))


def solution(mesh):
    placed = (P("ctx", "tp"), P("ctx", "tp"), P("ctx", "tp"), P("tp", "ctx"), P(), P())
    return jax.shard_map(
        shards, mesh=mesh, in_specs=placed, out_specs=P("ctx", "tp"), check_vma=False
    )
```

profile of v0, /device:TPU:1, one launch (start us, length us, event | category | flops | bytes accessed | tf_op | source)
XLA Modules:
  0.0 167.3 jit_solution(16374870759900681064)
XLA Ops:
  5.8 5.4 %collective-permute-done.rest_0_ = bf16[512,256]{1,0:T(8,128)(2,1)S(1)} collective-permute-done((bf16[512,256]{1,0:T(8,128)(2,1)S(1)}, bf16[512,256]{1,0:T(8,128)(2,1)S(1)}, u32[]{:S(2)}, u32[]{:S(2)}) %collective-permute-start) | collective-permute-done | bytes 262176 | tf_op jit(solution)/shard_map/ppermute | solution.py:291
  13.5 2.6 %collective-permute-start.2 = (bf16[512,256]{1,0:T(8,128)(2,1)S(1)}, bf16[512,256]{1,0:T(8,128)(2,1)S(1)}, u32[]{:S(2)}, u32[]{:S(2)}) collective-permute-start(bf16[512,256]{1,0:T(8,128)(2,1)S(1)} %get-tuple-element.130), channel_id=1, source_target_pairs={{0,16},{8,24},{16,0},{24,8},{32,48},{40,56},{48,32},{56,40},{64,80... | collective-permute-start | bytes 786440 | tf_op jit(solution)/shard_map/ppermute | solution.py:293
  17.2 1.8 %collective-permute-done.1.rest_3_ = bf16[512,256]{1,0:T(8,128)(2,1)S(1)} collective-permute-done((bf16[512,256]{1,0:T(8,128)(2,1)S(1)}, bf16[512,256]{1,0:T(8,128)(2,1)S(1)}, u32[]{:S(2)}, u32[]{:S(2)}) %collective-permute-start.1) | collective-permute-done | bytes 262176 | tf_op jit(solution)/shard_map/ppermute | solution.py:293
  19.7 5.4 %collective-permute-done.2.rest_2_ = bf16[512,256]{1,0:T(8,128)(2,1)S(1)} collective-permute-done((bf16[512,256]{1,0:T(8,128)(2,1)S(1)}, bf16[512,256]{1,0:T(8,128)(2,1)S(1)}, u32[]{:S(2)}, u32[]{:S(2)}) %collective-permute-start.2) | collective-permute-done | bytes 262176 | tf_op jit(solution)/shard_map/ppermute | solution.py:293
  34.5 5.9 %shard_map.64 = (bf16[256,1024]{1,0:T(8,128)(2,1)}, bf16[256,1024]{1,0:T(8,128)(2,1)}) custom-call(s32[8]{0:T(128)S(1)} %broadcast_subtract_fusion.firsts_ref, bf16[512,1024]{1,0:T(8,128)(2,1)S(1)} %copy-done.1, bf16[512,256]{1,0:T(8,128)(2,1)S(1)} %copy-done.3, bf16[512,256]{1,0:T(8,128)(2,1)S(1)} %copy-done.17, bf16[512,256]{1,0:T(8,128)(2,1)S(1)} %copy-done.15, ...), custom_call_target="tpu_custom_call" | custom-call | flops 1 | bytes 1 | tf_op jit(solution)/shard_map/pallas_call | solution.py:121
  40.4 6.3 %collective-permute-done.8.refs_8_ = bf16[1024,256]{1,0:T(8,128)(2,1)} collective-permute-done((bf16[1024,256]{1,0:T(8,128)(2,1)S(1)}, bf16[1024,256]{1,0:T(8,128)(2,1)}, u32[]{:S(2)}, u32[]{:S(2)}) %collective-permute-start.8) | collective-permute-done | bytes 524320 | tf_op jit(solution)/shard_map/ppermute | solution.py:304
  46.7 4.8 %collective-permute-start.13 = (bf16[256,1024]{1,0:T(8,128)(2,1)}, bf16[256,1024]{1,0:T(8,128)(2,1)}, u32[]{:S(2)}, u32[]{:S(2)}) collective-permute-start(bf16[256,1024]{1,0:T(8,128)(2,1)} %get-tuple-element.85.refs_0_), channel_id=1, source_target_pairs={{0,1},{1,0},{2,3},{3,2},{4,5},{5,4},{6,7},{7,6},{8,9},{9,8},{10,11... | collective-permute-start | bytes 1572872 | tf_op jit(solution)/shard_map/ppermute | solution.py:311
  54.1 4.3 %shard_map.65 = (bf16[512,256]{1,0:T(8,128)(2,1)S(1)}, bf16[512,256]{1,0:T(8,128)(2,1)S(1)}, bf16[512,256]{1,0:T(8,128)(2,1)S(1)}, bf16[512,256]{1,0:T(8,128)(2,1)S(1)}) custom-call(s32[1]{0:T(128)} %bitcast.2.turn_ref, bf16[256,1024]{1,0:T(8,128)(2,1)} %get-tuple-element.85.refs_0_, bf16[256,1024]{1,0:T(8,128)(2,1)} %get-tuple-element.84.refs_1_, ...), custom_call_target="tpu_custom_call" | custom-call | flops 1 | bytes 1 | tf_op jit(solution)/shard_map/pallas_call | solution.py:184
  58.5 6.4 %collective-permute-done.11.refs_0_ = bf16[256,1024]{1,0:T(8,128)(2,1)} collective-permute-done((bf16[256,1024]{1,0:T(8,128)(2,1)}, bf16[256,1024]{1,0:T(8,128)(2,1)}, u32[]{:S(2)}, u32[]{:S(2)}) %collective-permute-start.11) | collective-permute-done | bytes 524320 | tf_op jit(solution)/shard_map/ppermute | solution.py:314
  70.5 3.3 %collective-permute-start.18 = (bf16[512,256]{1,0:T(8,128)(2,1)S(1)}, bf16[512,256]{1,0:T(8,128)(2,1)S(1)}, u32[]{:S(2)}, u32[]{:S(2)}) collective-permute-start(bf16[512,256]{1,0:T(8,128)(2,1)S(1)} %get-tuple-element.89), channel_id=1, source_target_pairs={{0,4},{1,5},{2,6},{3,7},{4,0},{5,1},{6,2},{7,3},{8,12},{9,13},{10,... | collective-permute-start | bytes 786440 | tf_op jit(solution)/shard_map/ppermute | solution.py:211
  74.5 4.0 %shard_map.66 = (bf16[512,256]{1,0:T(8,128)(2,1)S(1)}, bf16[512,256]{1,0:T(8,128)(2,1)S(1)}, bf16[512,256]{1,0:T(8,128)(2,1)S(1)}, bf16[512,256]{1,0:T(8,128)(2,1)S(1)}) custom-call(s32[1]{0:T(128)} %bitcast.2.turn_ref, bf16[256,1024]{1,0:T(8,128)(2,1)} %collective-permute-done.11.refs_0_, bf16[256,1024]{1,0:T(8,128)(2,1)} %collective-permute-done.12.refs_1_, ...), custom_call_target="tpu_custom_call" | custom-call | flops 1 | bytes 1 | tf_op jit(solution)/shard_map/pallas_call | solution.py:184
  78.5 6.2 %collective-permute-done.18.refs_14_ = bf16[512,256]{1,0:T(8,128)(2,1)S(1)} collective-permute-done((bf16[512,256]{1,0:T(8,128)(2,1)S(1)}, bf16[512,256]{1,0:T(8,128)(2,1)S(1)}, u32[]{:S(2)}, u32[]{:S(2)}) %collective-permute-start.18) | collective-permute-done | bytes 262176 | tf_op jit(solution)/shard_map/ppermute | solution.py:211
  84.8 1.9 %collective-permute-start.22 = (bf16[256,1024]{1,0:T(8,128)(2,1)S(1)}, bf16[256,1024]{1,0:T(8,128)(2,1)S(1)}, u32[]{:S(2)}, u32[]{:S(2)}) collective-permute-start(bf16[256,1024]{1,0:T(8,128)(2,1)S(1)} %collective-permute-done.15.refs_0_), channel_id=1, source_target_pairs={{0,1},{1,0},{2,3},{3,2},{4,5},{5,4},{6,7},{7,6},{8,9},{9,8},{10,11... | collective-permute-start | bytes 1572872 | tf_op jit(solution)/shard_map/ppermute | solution.py:311
  89.4 2.1 %collective-permute-start.27 = (bf16[512,256]{1,0:T(8,128)(2,1)S(1)}, bf16[512,256]{1,0:T(8,128)(2,1)S(1)}, u32[]{:S(2)}, u32[]{:S(2)}) collective-permute-start(bf16[512,256]{1,0:T(8,128)(2,1)S(1)} %get-tuple-element.102), channel_id=1, source_target_pairs={{0,4},{1,5},{2,6},{3,7},{4,0},{5,1},{6,2},{7,3},{8,12},{9,13},{10,... | collective-permute-start | bytes 786440 | tf_op jit(solution)/shard_map/ppermute | solution.py:211
  92.3 4.6 %shard_map.67 = (bf16[512,256]{1,0:T(8,128)(2,1)S(1)}, bf16[512,256]{1,0:T(8,128)(2,1)S(1)}, bf16[512,256]{1,0:T(8,128)(2,1)}, bf16[512,256]{1,0:T(8,128)(2,1)}, bf16[512,256]{1,0:T(8,128)(2,1)S(1)}) custom-call(s32[1]{0:T(128)} %bitcast.2.turn_ref, bf16[256,1024]{1,0:T(8,128)(2,1)S(1)} %collective-permute-done.15.refs_0_, ...), custom_call_target="tpu_custom_call" | custom-call | flops 1 | bytes 1 | tf_op jit(solution)/shard_map/pallas_call | solution.py:184
  97.6 4.9 %collective-permute-done.27.refs_14_ = bf16[512,256]{1,0:T(8,128)(2,1)S(1)} collective-permute-done((bf16[512,256]{1,0:T(8,128)(2,1)S(1)}, bf16[512,256]{1,0:T(8,128)(2,1)S(1)}, u32[]{:S(2)}, u32[]{:S(2)}) %collective-permute-start.27) | collective-permute-done | bytes 262176 | tf_op jit(solution)/shard_map/ppermute | solution.py:211
  105.8 2.3 %collective-permute-start.32 = (bf16[512,256]{1,0:T(8,128)(2,1)}, bf16[512,256]{1,0:T(8,128)(2,1)}, u32[]{:S(2)}, u32[]{:S(2)}) collective-permute-start(bf16[512,256]{1,0:T(8,128)(2,1)} %get-tuple-element.113), channel_id=1, source_target_pairs={{0,4},{1,5},{2,6},{3,7},{4,0},{5,1},{6,2},{7,3},{8,12},{9,13},{10,... | collective-permute-start | bytes 786440 | tf_op jit(solution)/shard_map/ppermute | solution.py:211
  108.5 4.7 %shard_map.68 = (bf16[512,256]{1,0:T(8,128)(2,1)S(1)}, bf16[512,256]{1,0:T(8,128)(2,1)}, bf16[512,256]{1,0:T(8,128)(2,1)}, bf16[512,256]{1,0:T(8,128)(2,1)}, bf16[512,256]{1,0:T(8,128)(2,1)S(1)}) custom-call(s32[1]{0:T(128)} %bitcast.2.turn_ref, bf16[256,1024]{1,0:T(8,128)(2,1)S(1)} %collective-permute-done.24.refs_0_, ...), custom_call_target="tpu_custom_call" | custom-call | flops 1 | bytes 1 | tf_op jit(solution)/shard_map/pallas_call | solution.py:184
  120.1 6.1 %collective-permute-done.34.refs_7_ = bf16[512,256]{1,0:T(8,128)(2,1)S(1)} collective-permute-done((bf16[512,256]{1,0:T(8,128)(2,1)}, bf16[512,256]{1,0:T(8,128)(2,1)S(1)}, u32[]{:S(2)}, u32[]{:S(2)}) %collective-permute-start.34) | collective-permute-done | bytes 262176 | tf_op jit(solution)/shard_map/ppermute | solution.py:211
  126.2 4.8 %collective-permute-done.35.refs_8_ = bf16[512,256]{1,0:T(8,128)(2,1)S(1)} collective-permute-done((bf16[512,256]{1,0:T(8,128)(2,1)}, bf16[512,256]{1,0:T(8,128)(2,1)S(1)}, u32[]{:S(2)}, u32[]{:S(2)}) %collective-permute-start.35) | collective-permute-done | bytes 262176 | tf_op jit(solution)/shard_map/ppermute | solution.py:211
  134.8 2.6 %shard_map.69 = bf16[16,4,32,256]{3,2,1,0:T(8,128)(2,1)} custom-call(s32[1]{0:T(128)} %bitcast.1.y_ref, s32[4,16]{1,0:T(4,128)S(1)} %constant_dynamic-slice_fusion.2.sources_ref, bf16[512,256]{1,0:T(8,128)(2,1)S(1)} %copy-done.5, bf16[512,256]{1,0:T(8,128)(2,1)S(1)} %copy-done.11, bf16[512,256]{1,0:T(8,128)(2,1)S(1)} %get-tuple-element.119.refs_2_, ...), custom_call_target="tpu_custom_call" | custom-call | flops 1 | bytes 1 | tf_op jit(solution)/shard_map/pallas_call | solution.py:239
  137.3 8.9 %all-to-all-start = ((bf16[16,4,32,256]{3,2,1,0:T(8,128)(2,1)}), bf16[16,4,32,256]{3,2,1,0:T(8,128)(2,1)S(1)}, u32[]{:S(2)}, u32[]{:S(2)}) async-start(bf16[16,4,32,256]{3,2,1,0:T(8,128)(2,1)} %shard_map.69), calls=%async_computation | async-start | bytes 2097152 | tf_op jit(solution)/shard_map/all_to_all | solution.py:337
  146.3 15.2 %all-to-all-done = bf16[16,4,32,256]{3,2,1,0:T(8,128)(2,1)S(1)} async-done(((bf16[16,4,32,256]{3,2,1,0:T(8,128)(2,1)}), bf16[16,4,32,256]{3,2,1,0:T(8,128)(2,1)S(1)}, u32[]{:S(2)}, u32[]{:S(2)}) %all-to-all-start) | async-done | bytes 1048608 | tf_op jit(solution)/shard_map/all_to_all | solution.py:337
  161.5 3.2 %collective-permute-start.37 = (bf16[4,2,4,32,256]{4,3,2,1,0:T(8,128)(2,1)S(1)}, bf16[4,2,4,32,256]{4,3,2,1,0:T(8,128)(2,1)S(1)}, u32[]{:S(2)}, u32[]{:S(2)}) collective-permute-start(bf16[4,2,4,32,256]{4,3,2,1,0:T(8,128)(2,1)S(1)} %dynamic-slice_bitcast_fusion), channel_id=1, source_target_pairs={{0,1},{1,0},{2,3},{3,2},{4,5},{5,4},{6,7},{7,6},{8,9},{9,8},{10,11... | collective-permute-start | bytes 1572872 | tf_op jit(solution)/shard_map/ppermute | solution.py:311
  (111 shorter events, 49.6 us)
Async XLA Ops:
  4.4 23.5 %collective-permute-start.4 = (bf16[1024,256]{1,0:T(8,128)(2,1)S(1)}, bf16[1024,256]{1,0:T(8,128)(2,1)S(1)}, u32[]{:S(2)}, u32[]{:S(2)}) collective-permute-start(bf16[1024,256]{1,0:T(8,128)(2,1)S(1)} %get-tuple-element.75.refs_4_), channel_id=1, source_target_pairs={{0,96},{8,104},{16,112},{24,120},{32,0},{40,8},{48,16},{56,24},{64... | collective-permute-start | bytes 1572872 | tf_op jit(solution)/shard_map/ppermute | solution.py:301
  5.7 22.1 %collective-permute-start.6 = (bf16[1024,256]{1,0:T(8,128)(2,1)S(1)}, bf16[1024,256]{1,0:T(8,128)(2,1)S(1)}, u32[]{:S(2)}, u32[]{:S(2)}) collective-permute-start(bf16[1024,256]{1,0:T(8,128)(2,1)S(1)} %collective-permute-done.5.refs_5_), channel_id=1, source_target_pairs={{0,32},{8,40},{16,48},{24,56},{32,64},{40,72},{48,80},{56,88},{64,... | collective-permute-start | bytes 1572872 | tf_op jit(solution)/shard_map/ppermute | solution.py:302
  13.5 11.6 %collective-permute-start.2 = (bf16[512,256]{1,0:T(8,128)(2,1)S(1)}, bf16[512,256]{1,0:T(8,128)(2,1)S(1)}, u32[]{:S(2)}, u32[]{:S(2)}) collective-permute-start(bf16[512,256]{1,0:T(8,128)(2,1)S(1)} %get-tuple-element.130), channel_id=1, source_target_pairs={{0,16},{8,24},{16,0},{24,8},{32,48},{40,56},{48,32},{56,40},{64,80... | collective-permute-start | bytes 786440 | tf_op jit(solution)/shard_map/ppermute | solution.py:293
  19.7 20.7 %collective-permute-start.10 = (bf16[1024,256]{1,0:T(8,128)(2,1)S(1)}, bf16[1024,256]{1,0:T(8,128)(2,1)S(1)}, u32[]{:S(2)}, u32[]{:S(2)}) collective-permute-start(bf16[1024,256]{1,0:T(8,128)(2,1)S(1)} %get-tuple-element.75.refs_4_), channel_id=1, source_target_pairs={{0,32},{8,40},{16,48},{24,56},{32,64},{40,72},{48,80},{56,88},{64,... | collective-permute-start | bytes 1572872 | tf_op jit(solution)/shard_map/ppermute | solution.py:302
  25.8 14.6 %collective-permute-start.7 = (bf16[1024,256]{1,0:T(8,128)(2,1)S(1)}, bf16[1024,256]{1,0:T(8,128)(2,1)S(1)}, u32[]{:S(2)}, u32[]{:S(2)}) collective-permute-start(bf16[1024,256]{1,0:T(8,128)(2,1)S(1)} %collective-permute-done.5.refs_5_), channel_id=1, source_target_pairs={{0,96},{8,104},{16,112},{24,120},{32,0},{40,8},{48,16},{56,24},{64... | collective-permute-start | bytes 1572872 | tf_op jit(solution)/shard_map/ppermute | solution.py:301
  27.8 18.8 %collective-permute-start.8 = (bf16[1024,256]{1,0:T(8,128)(2,1)S(1)}, bf16[1024,256]{1,0:T(8,128)(2,1)}, u32[]{:S(2)}, u32[]{:S(2)}) collective-permute-start(bf16[1024,256]{1,0:T(8,128)(2,1)S(1)} %collective-permute-done.4.refs_6_), channel_id=1, source_target_pairs={{0,96},{8,104},{16,112},{24,120},{32,0},{40,8},{48,16},{56,24},{64... | collective-permute-start | bytes 1572872 | tf_op jit(solution)/shard_map/ppermute | solution.py:304
  28.4 18.3 %collective-permute-start.9 = (bf16[1024,256]{1,0:T(8,128)(2,1)S(1)}, bf16[1024,256]{1,0:T(8,128)(2,1)}, u32[]{:S(2)}, u32[]{:S(2)}) collective-permute-start(bf16[1024,256]{1,0:T(8,128)(2,1)S(1)} %collective-permute-done.6.refs_11_), channel_id=1, source_target_pairs={{0,32},{8,40},{16,48},{24,56},{32,64},{40,72},{48,80},{56,88},{64,... | collective-permute-start | bytes 1572872 | tf_op jit(solution)/shard_map/ppermute | solution.py:305
  51.5 13.3 %collective-permute-start.11 = (bf16[256,1024]{1,0:T(8,128)(2,1)}, bf16[256,1024]{1,0:T(8,128)(2,1)}, u32[]{:S(2)}, u32[]{:S(2)}) collective-permute-start(bf16[256,1024]{1,0:T(8,128)(2,1)} %get-tuple-element.85.refs_0_), channel_id=1, source_target_pairs={{0,24},{8,0},{16,8},{24,16},{32,56},{40,32},{48,40},{56,48},{64,88... | collective-permute-start | bytes 1572872 | tf_op jit(solution)/shard_map/ppermute | solution.py:314
  51.5 14.5 %collective-permute-start.12 = (bf16[256,1024]{1,0:T(8,128)(2,1)}, bf16[256,1024]{1,0:T(8,128)(2,1)}, u32[]{:S(2)}, u32[]{:S(2)}) collective-permute-start(bf16[256,1024]{1,0:T(8,128)(2,1)} %get-tuple-element.84.refs_1_), channel_id=1, source_target_pairs={{0,8},{8,16},{16,24},{24,0},{32,40},{40,48},{48,56},{56,32},{64,72... | collective-permute-start | bytes 1572872 | tf_op jit(solution)/shard_map/ppermute | solution.py:314
  67.4 17.4 %collective-permute-start.15 = (bf16[256,1024]{1,0:T(8,128)(2,1)}, bf16[256,1024]{1,0:T(8,128)(2,1)S(1)}, u32[]{:S(2)}, u32[]{:S(2)}) collective-permute-start(bf16[256,1024]{1,0:T(8,128)(2,1)} %get-tuple-element.84.refs_1_), channel_id=1, source_target_pairs={{0,24},{8,0},{16,8},{24,16},{32,56},{40,32},{48,40},{56,48},{64,88... | collective-permute-start | bytes 1572872 | tf_op jit(solution)/shard_map/ppermute | solution.py:314
  67.4 17.4 %collective-permute-start.16 = (bf16[256,1024]{1,0:T(8,128)(2,1)}, bf16[256,1024]{1,0:T(8,128)(2,1)S(1)}, u32[]{:S(2)}, u32[]{:S(2)}) collective-permute-start(bf16[256,1024]{1,0:T(8,128)(2,1)} %get-tuple-element.85.refs_0_), channel_id=1, source_target_pairs={{0,8},{8,16},{16,24},{24,0},{32,40},{40,48},{48,56},{56,32},{64,72... | collective-permute-start | bytes 1572872 | tf_op jit(solution)/shard_map/ppermute | solution.py:314
  70.5 14.2 %collective-permute-start.18 = (bf16[512,256]{1,0:T(8,128)(2,1)S(1)}, bf16[512,256]{1,0:T(8,128)(2,1)S(1)}, u32[]{:S(2)}, u32[]{:S(2)}) collective-permute-start(bf16[512,256]{1,0:T(8,128)(2,1)S(1)} %get-tuple-element.89), channel_id=1, source_target_pairs={{0,4},{1,5},{2,6},{3,7},{4,0},{5,1},{6,2},{7,3},{8,12},{9,13},{10,... | collective-permute-start | bytes 786440 | tf_op jit(solution)/shard_map/ppermute | solution.py:211
  73.8 11.0 %collective-permute-start.19 = (bf16[512,256]{1,0:T(8,128)(2,1)S(1)}, bf16[512,256]{1,0:T(8,128)(2,1)S(1)}, u32[]{:S(2)}, u32[]{:S(2)}) collective-permute-start(bf16[512,256]{1,0:T(8,128)(2,1)S(1)} %get-tuple-element.90), channel_id=1, source_target_pairs={{0,6},{1,7},{2,0},{3,1},{4,2},{5,3},{6,4},{7,5},{8,14},{9,15},{10,... | collective-permute-start | bytes 786440 | tf_op jit(solution)/shard_map/ppermute | solution.py:211
  86.9 16.1 %collective-permute-start.24 = (bf16[256,1024]{1,0:T(8,128)(2,1)}, bf16[256,1024]{1,0:T(8,128)(2,1)S(1)}, u32[]{:S(2)}, u32[]{:S(2)}) collective-permute-start(bf16[256,1024]{1,0:T(8,128)(2,1)} %collective-permute-done.11.refs_0_), channel_id=1, source_target_pairs={{0,24},{8,0},{16,8},{24,16},{32,56},{40,32},{48,40},{56,48},{64,88... | collective-permute-start | bytes 1572872 | tf_op jit(solution)/shard_map/ppermute | solution.py:314
  88.1 14.9 %collective-permute-start.25 = (bf16[256,1024]{1,0:T(8,128)(2,1)}, bf16[256,1024]{1,0:T(8,128)(2,1)S(1)}, u32[]{:S(2)}, u32[]{:S(2)}) collective-permute-start(bf16[256,1024]{1,0:T(8,128)(2,1)} %collective-permute-done.12.refs_1_), channel_id=1, source_target_pairs={{0,8},{8,16},{16,24},{24,0},{32,40},{40,48},{48,56},{56,32},{64,72... | collective-permute-start | bytes 1572872 | tf_op jit(solution)/shard_map/ppermute | solution.py:314
  89.4 13.1 %collective-permute-start.27 = (bf16[512,256]{1,0:T(8,128)(2,1)S(1)}, bf16[512,256]{1,0:T(8,128)(2,1)S(1)}, u32[]{:S(2)}, u32[]{:S(2)}) collective-permute-start(bf16[512,256]{1,0:T(8,128)(2,1)S(1)} %get-tuple-element.102), channel_id=1, source_target_pairs={{0,4},{1,5},{2,6},{3,7},{4,0},{5,1},{6,2},{7,3},{8,12},{9,13},{10,... | collective-permute-start | bytes 786440 | tf_op jit(solution)/shard_map/ppermute | solution.py:211
  91.5 11.5 %collective-permute-start.28 = (bf16[512,256]{1,0:T(8,128)(2,1)S(1)}, bf16[512,256]{1,0:T(8,128)(2,1)S(1)}, u32[]{:S(2)}, u32[]{:S(2)}) collective-permute-start(bf16[512,256]{1,0:T(8,128)(2,1)S(1)} %get-tuple-element.103), channel_id=1, source_target_pairs={{0,6},{1,7},{2,0},{3,1},{4,2},{5,3},{6,4},{7,5},{8,14},{9,15},{10,... | collective-permute-start | bytes 786440 | tf_op jit(solution)/shard_map/ppermute | solution.py:211
  104.6 11.9 %collective-permute-start.31 = (bf16[512,256]{1,0:T(8,128)(2,1)S(1)}, bf16[512,256]{1,0:T(8,128)(2,1)S(1)}, u32[]{:S(2)}, u32[]{:S(2)}) collective-permute-start(bf16[512,256]{1,0:T(8,128)(2,1)S(1)} %get-tuple-element.112), channel_id=1, source_target_pairs={{0,2},{1,3},{2,4},{3,5},{4,6},{5,7},{6,0},{7,1},{8,10},{9,11},{10,... | collective-permute-start | bytes 786440 | tf_op jit(solution)/shard_map/ppermute | solution.py:211
  105.8 14.0 %collective-permute-start.32 = (bf16[512,256]{1,0:T(8,128)(2,1)}, bf16[512,256]{1,0:T(8,128)(2,1)}, u32[]{:S(2)}, u32[]{:S(2)}) collective-permute-start(bf16[512,256]{1,0:T(8,128)(2,1)} %get-tuple-element.113), channel_id=1, source_target_pairs={{0,4},{1,5},{2,6},{3,7},{4,0},{5,1},{6,2},{7,3},{8,12},{9,13},{10,... | collective-permute-start | bytes 786440 | tf_op jit(solution)/shard_map/ppermute | solution.py:211
  108.1 11.9 %collective-permute-start.33 = (bf16[512,256]{1,0:T(8,128)(2,1)}, bf16[512,256]{1,0:T(8,128)(2,1)}, u32[]{:S(2)}, u32[]{:S(2)}) collective-permute-start(bf16[512,256]{1,0:T(8,128)(2,1)} %get-tuple-element.114), channel_id=1, source_target_pairs={{0,6},{1,7},{2,0},{3,1},{4,2},{5,3},{6,4},{7,5},{8,14},{9,15},{10,... | collective-permute-start | bytes 786440 | tf_op jit(solution)/shard_map/ppermute | solution.py:211
  114.7 11.5 %collective-permute-start.34 = (bf16[512,256]{1,0:T(8,128)(2,1)}, bf16[512,256]{1,0:T(8,128)(2,1)S(1)}, u32[]{:S(2)}, u32[]{:S(2)}) collective-permute-start(bf16[512,256]{1,0:T(8,128)(2,1)} %get-tuple-element.116), channel_id=1, source_target_pairs={{0,2},{1,3},{2,4},{3,5},{4,6},{5,7},{6,0},{7,1},{8,10},{9,11},{10,... | collective-permute-start | bytes 786440 | tf_op jit(solution)/shard_map/ppermute | solution.py:211
  115.8 15.2 %collective-permute-start.35 = (bf16[512,256]{1,0:T(8,128)(2,1)}, bf16[512,256]{1,0:T(8,128)(2,1)S(1)}, u32[]{:S(2)}, u32[]{:S(2)}) collective-permute-start(bf16[512,256]{1,0:T(8,128)(2,1)} %get-tuple-element.117), channel_id=1, source_target_pairs={{0,4},{1,5},{2,6},{3,7},{4,0},{5,1},{6,2},{7,3},{8,12},{9,13},{10,... | collective-permute-start | bytes 786440 | tf_op jit(solution)/shard_map/ppermute | solution.py:211
  117.2 13.8 %collective-permute-start.36 = (bf16[512,256]{1,0:T(8,128)(2,1)}, bf16[512,256]{1,0:T(8,128)(2,1)S(1)}, u32[]{:S(2)}, u32[]{:S(2)}) collective-permute-start(bf16[512,256]{1,0:T(8,128)(2,1)} %get-tuple-element.118), channel_id=1, source_target_pairs={{0,6},{1,7},{2,0},{3,1},{4,2},{5,3},{6,4},{7,5},{8,14},{9,15},{10,... | collective-permute-start | bytes 786440 | tf_op jit(solution)/shard_map/ppermute | solution.py:211
  137.3 24.2 %all-to-all-start = ((bf16[16,4,32,256]{3,2,1,0:T(8,128)(2,1)}), bf16[16,4,32,256]{3,2,1,0:T(8,128)(2,1)S(1)}, u32[]{:S(2)}, u32[]{:S(2)}) async-start(bf16[16,4,32,256]{3,2,1,0:T(8,128)(2,1)} %shard_map.69), calls=%async_computation | async-start | bytes 2097152 | tf_op jit(solution)/shard_map/all_to_all | solution.py:337
  (36 other events, 254.8 us)
where the time goes:
time: 170 us; the launch traced here: 167 us
  waiting for transfers between devices  68.1 us (40%)
  starting transfers between devices  55.8 us (33%)
  Pallas kernels  27.1 us (16%)
  local copies, waits for them, and re-layouts  15.9 us (9%)
    ppermute x12, waiting for transfers between devices, spread_z(): lax.ppermute(pieces[e], 'tp', z_shift(e))  23.8 us
    pallas_call x4, Pallas kernels, project(): pl.pallas_call(functools.partial(project_kernel, count), in_specs=[pl.Blo...  17.6 us
    ppermute x12, starting transfers between devices, spread_z(): lax.ppermute(pieces[e], 'tp', z_shift(e))  17 us
    all_to_all x1, waiting for transfers between devices, shards(): lax.all_to_all(outgoing, 'ctx', split_axis=0, concat_axis=0, tiled=True)  15.2 us
    unnamed x43, local copies, waits for them, and re-layouts  14.5 us
    ppermute x9, starting transfers between devices, swap(): return lax.ppermute(a, 'tp', CORES)  13.1 us
    all_to_all x1, starting transfers between devices, shards(): lax.all_to_all(outgoing, 'ctx', split_axis=0, concat_axis=0, tiled=True)  8.93 us
    ppermute x6, waiting for transfers between devices, along(): return lax.ppermute(a, 'ctx', grid_shift(0, -steps))  7.57 us
  transfers between devices with their start and end apart: 39, of which 18 were waited for; matrix products, arithmetic and copies ran while one was open for 0% of the time, Pallas kernels for 14%

commit v1 on v0

--- a/solution.py
+++ b/solution.py
@@ -137,7 +137,7 @@
             ],
         ),
         out_shape=[jax.ShapeDtypeStruct((TILE, width), jnp.bfloat16)] * (tokens // TILE),
-        compiler_params=pltpu.CompilerParams(vmem_limit_bytes=24 * 1024 * 1024),
+        compiler_params=pltpu.CompilerParams(vmem_limit_bytes=65300 * 1024),
         cost_estimate=pl.CostEstimate(
             flops=1, bytes_accessed=1, transcendentals=0
         ),
@@ -243,7 +243,7 @@
         out_specs=pl.BlockSpec(shape, lambda i: (0, 0, 0, 0)),
         out_shape=jax.ShapeDtypeStruct(shape, jnp.bfloat16),
         scratch_shapes=[pltpu.VMEM((SIDE, owners, block, part), jnp.bfloat16)],
-        compiler_params=pltpu.CompilerParams(vmem_limit_bytes=16 * 1024 * 1024),
+        compiler_params=pltpu.CompilerParams(vmem_limit_bytes=60 * 1024 * 1024),
         cost_estimate=pl.CostEstimate(flops=1, bytes_accessed=1, transcendentals=0),
     )(y, sources, *terms)
 
@@ -299,7 +299,8 @@
     given = lax.dynamic_slice_in_dim(out_weight, (1 - core) * part, part, axis=1)
     taken = lax.ppermute(given, "tp", CORES)
     kept_next, taken_next = [lax.ppermute(a, "ctx", grid_shift(-1, 0)) for a in (kept, taken)]
-    taken_last, kept_last = [lax.ppermute(a, "ctx", grid_shift(1, 0)) for a in (taken, kept)]
+    taken_last = lax.ppermute(after(taken, above), "ctx", grid_shift(1, 0))
+    kept_last = lax.ppermute(after(kept, above), "ctx", grid_shift(1, 0))
     near, (kept_next, taken_last) = meet(near, [kept_next, taken_last])
     kept_far = lax.ppermute(kept_next, "ctx", grid_shift(-1, 0))
     taken_far = lax.ppermute(taken_last, "ctx", grid_shift(1, 0))
@@ -323,10 +324,10 @@
     swaps = [swap(head), swap(tail)]
     outer = [along(head, 1), along(tail, 3)]
     own, _ = terms([head, tail], swaps)
-    outer, pair, _ = meet(outer, [tail, head], own[:1])
+    outer, pair, _ = meet(outer, [tail, head], own[:1] + own[2:3])
     inner = [along(pair[0], 1), along(pair[1], 3)]
     outer_terms, _ = terms(outer)
-    inner, outer, own, _ = meet(inner, outer, own, outer_terms[:1])
+    inner, outer, own, _ = meet(inner, outer, own, outer_terms[:1] + outer_terms[2:3])
     far = [along(outer[0], 1), along(outer[1], 3)]
     inner_terms, own = terms(inner, finished=own)
     far, outer_terms, _ = meet(far, outer_terms, inner_terms[:1])

time: 170 us -> 164 us (0.965); the launches traced: 167 us -> 164 us
  local copies, waits for them, and re-layouts: 15.9 us -> 5.86 us
  waiting for transfers between devices: 68.1 us -> 72.9 us
  Pallas kernels: 27.1 us -> 31.7 us
  starting transfers between devices: 55.8 us -> 52.4 us
    unnamed x43 -> x33, local copies, waits for them, and re-layouts: 14.5 us -> 3.09 us
    ppermute x12, waiting for transfers between devices: 23.8 us -> 18.4 us  [spread_z(): lax.ppermute(pieces[e], 'tp', z_shift(e))]
    ppermute x1, waiting for transfers between devices: 6.26 us -> 10.9 us  [shards(): kept_far = lax.ppermute(kept_next, 'ctx', grid_shift(-1, 0))]
    all_to_all x1, starting transfers between devices: 8.93 us -> 4.88 us  [shards(): lax.all_to_all(outgoing, 'ctx', split_axis=0, concat_axis=0, tiled=True)]
    ppermute x6, waiting for transfers between devices: 7.57 us -> 11.5 us  [along(): return lax.ppermute(a, 'ctx', grid_shift(0, -steps))]
    pallas_call x4, Pallas kernels: 17.6 us -> 20 us  [project(): pl.pallas_call(functools.partial(project_kernel, count), in_specs=[pl.Blo...]
    ppermute x3, waiting for transfers between devices: 7.18 us -> 9.03 us  [shards(): lax.ppermute(jnp.where(y + k < SIDE, both, above), 'ctx', grid_shift(0, k))]
  transfers between devices with their start and end apart: 39 -> 39, of which waited for: 18 -> 22; matrix products, arithmetic and copies ran while one was open for 0% -> 1% of each run, Pallas kernels for 14% -> 17%
where the time goes in v1:
time: 164 us
  waiting for transfers between devices  72.9 us (44%)
  starting transfers between devices  52.4 us (32%)
  Pallas kernels  31.7 us (19%)
  local copies, waits for them, and re-layouts  5.86 us (4%)
    pallas_call x4, Pallas kernels, project(): pl.pallas_call(functools.partial(project_kernel, count), in_specs=[pl.Blo...  20 us
    ppermute x12, waiting for transfers between devices, spread_z(): lax.ppermute(pieces[e], 'tp', z_shift(e))  18.4 us
    ppermute x12, starting transfers between devices, spread_z(): lax.ppermute(pieces[e], 'tp', z_shift(e))  17.9 us
    all_to_all x1, waiting for transfers between devices, shards(): lax.all_to_all(outgoing, 'ctx', split_axis=0, concat_axis=0, tiled=True)  14.9 us
    ppermute x6, waiting for transfers between devices, along(): return lax.ppermute(a, 'ctx', grid_shift(0, -steps))  11.5 us
    ppermute x9, starting transfers between devices, swap(): return lax.ppermute(a, 'tp', CORES)  11.4 us
    ppermute x1, waiting for transfers between devices, shards(): kept_far = lax.ppermute(kept_next, 'ctx', grid_shift(-1, 0))  10.9 us
    ppermute x3, waiting for transfers between devices, shards(): lax.ppermute(jnp.where(y + k < SIDE, both, above), 'ctx', grid_shift(0, k))  9.03 us
  transfers between devices with their start and end apart: 39, of which 22 were waited for; matrix products, arithmetic and copies ran while one was open for 1% of the time, Pallas kernels for 17%

profile of v1, /device:TPU:1, one launch (start us, length us, event | category | flops | bytes accessed | tf_op | source)
XLA Modules:
  0.0 163.9 jit_solution(7412331727219067383)
XLA Ops:
  6.5 5.5 %collective-permute-done.rest_0_ = bf16[512,256]{1,0:T(8,128)(2,1)S(1)} collective-permute-done((bf16[512,256]{1,0:T(8,128)(2,1)S(1)}, bf16[512,256]{1,0:T(8,128)(2,1)S(1)}, u32[]{:S(2)}, u32[]{:S(2)}) %collective-permute-start) | collective-permute-done | bytes 262176 | tf_op jit(solution)/shard_map/ppermute | solution.py:291
  14.4 2.6 %collective-permute-start.2 = (bf16[512,256]{1,0:T(8,128)(2,1)S(1)}, bf16[512,256]{1,0:T(8,128)(2,1)}, u32[]{:S(2)}, u32[]{:S(2)}) collective-permute-start(bf16[512,256]{1,0:T(8,128)(2,1)S(1)} %get-tuple-element.134), channel_id=1, source_target_pairs={{0,16},{8,24},{16,0},{24,8},{32,48},{40,56},{48,32},{56,40},{64,80... | collective-permute-start | bytes 786440 | tf_op jit(solution)/shard_map/ppermute | solution.py:293
  18.1 2.9 %collective-permute-done.1.rest_3_ = bf16[512,256]{1,0:T(8,128)(2,1)} collective-permute-done((bf16[512,256]{1,0:T(8,128)(2,1)S(1)}, bf16[512,256]{1,0:T(8,128)(2,1)}, u32[]{:S(2)}, u32[]{:S(2)}) %collective-permute-start.1) | collective-permute-done | bytes 262176 | tf_op jit(solution)/shard_map/ppermute | solution.py:293
  21.4 6.1 %collective-permute-done.2.rest_2_ = bf16[512,256]{1,0:T(8,128)(2,1)} collective-permute-done((bf16[512,256]{1,0:T(8,128)(2,1)S(1)}, bf16[512,256]{1,0:T(8,128)(2,1)}, u32[]{:S(2)}, u32[]{:S(2)}) %collective-permute-start.2) | collective-permute-done | bytes 262176 | tf_op jit(solution)/shard_map/ppermute | solution.py:293
  31.7 7.5 %shard_map.64 = (bf16[256,1024]{1,0:T(8,128)(2,1)}, bf16[256,1024]{1,0:T(8,128)(2,1)}) custom-call(s32[8]{0:T(128)} %broadcast_subtract_fusion.firsts_ref, bf16[512,1024]{1,0:T(8,128)(2,1)} %q_ref.1, bf16[512,256]{1,0:T(8,128)(2,1)} %copy-done.6, bf16[512,256]{1,0:T(8,128)(2,1)} %collective-permute-done.3.rest_1_, ...), custom_call_target="tpu_custom_call" | custom-call | flops 1 | bytes 1 | tf_op jit(solution)/shard_map/pallas_call | solution.py:121
  39.1 10.9 %collective-permute-done.8.refs_8_ = bf16[1024,256]{1,0:T(8,128)(2,1)} collective-permute-done((bf16[1024,256]{1,0:T(8,128)(2,1)}, bf16[1024,256]{1,0:T(8,128)(2,1)}, u32[]{:S(2)}, u32[]{:S(2)}) %collective-permute-start.8) | collective-permute-done | bytes 524320 | tf_op jit(solution)/shard_map/ppermute | solution.py:305
  50.0 3.4 %collective-permute-start.13 = (bf16[256,1024]{1,0:T(8,128)(2,1)}, bf16[256,1024]{1,0:T(8,128)(2,1)S(1)}, u32[]{:S(2)}, u32[]{:S(2)}) collective-permute-start(bf16[256,1024]{1,0:T(8,128)(2,1)} %get-tuple-element.90.refs_0_), channel_id=1, source_target_pairs={{0,1},{1,0},{2,3},{3,2},{4,5},{5,4},{6,7},{7,6},{8,9},{9,8},{10,11... | collective-permute-start | bytes 1572872 | tf_op jit(solution)/shard_map/ppermute | solution.py:312
  55.9 4.9 %shard_map.65 = (bf16[512,256]{1,0:T(8,128)(2,1)S(1)}, bf16[512,256]{1,0:T(8,128)(2,1)S(1)}, bf16[512,256]{1,0:T(8,128)(2,1)S(1)}, bf16[512,256]{1,0:T(8,128)(2,1)S(1)}) custom-call(s32[1]{0:T(128)} %bitcast.2.turn_ref, bf16[256,1024]{1,0:T(8,128)(2,1)} %get-tuple-element.90.refs_0_, bf16[256,1024]{1,0:T(8,128)(2,1)} %get-tuple-element.89.refs_1_, ...), custom_call_target="tpu_custom_call" | custom-call | flops 1 | bytes 1 | tf_op jit(solution)/shard_map/pallas_call | solution.py:184
  60.8 3.7 %collective-permute-start.15 = (bf16[512,256]{1,0:T(8,128)(2,1)S(1)}, bf16[512,256]{1,0:T(8,128)(2,1)S(1)}, u32[]{:S(2)}, u32[]{:S(2)}) collective-permute-start(bf16[512,256]{1,0:T(8,128)(2,1)S(1)} %get-tuple-element.88), channel_id=1, source_target_pairs={{0,4},{1,5},{2,6},{3,7},{4,0},{5,1},{6,2},{7,3},{8,12},{9,13},{10,... | collective-permute-start | bytes 786440 | tf_op jit(solution)/shard_map/ppermute | solution.py:211
  67.5 3.3 %collective-permute-done.15.refs_14_ = bf16[512,256]{1,0:T(8,128)(2,1)S(1)} collective-permute-done((bf16[512,256]{1,0:T(8,128)(2,1)S(1)}, bf16[512,256]{1,0:T(8,128)(2,1)S(1)}, u32[]{:S(2)}, u32[]{:S(2)}) %collective-permute-start.15) | collective-permute-done | bytes 262176 | tf_op jit(solution)/shard_map/ppermute | solution.py:211
  76.4 4.6 %shard_map.66 = (bf16[512,256]{1,0:T(8,128)(2,1)S(1)}, bf16[512,256]{1,0:T(8,128)(2,1)S(1)}, bf16[512,256]{1,0:T(8,128)(2,1)S(1)}, bf16[512,256]{1,0:T(8,128)(2,1)S(1)}) custom-call(s32[1]{0:T(128)} %bitcast.2.turn_ref, bf16[256,1024]{1,0:T(8,128)(2,1)S(1)} %collective-permute-done.11.refs_0_, bf16[256,1024]{1,0:T(8,128)(2,1)S(1)} %collective-permute-done.12.refs_1_, ...), custom_call_target="tpu_custom_call" | custom-call | flops 1 | bytes 1 | tf_op jit(solution)/shard_map/pallas_call | solution.py:184
  82.4 2.6 %collective-permute-done.16.refs_0_ = bf16[256,1024]{1,0:T(8,128)(2,1)S(1)} collective-permute-done((bf16[256,1024]{1,0:T(8,128)(2,1)}, bf16[256,1024]{1,0:T(8,128)(2,1)S(1)}, u32[]{:S(2)}, u32[]{:S(2)}) %collective-permute-start.16) | collective-permute-done | bytes 524320 | tf_op jit(solution)/shard_map/ppermute | solution.py:315
  86.1 3.1 %collective-permute-done.22.refs_14_ = bf16[512,256]{1,0:T(8,128)(2,1)S(1)} collective-permute-done((bf16[512,256]{1,0:T(8,128)(2,1)S(1)}, bf16[512,256]{1,0:T(8,128)(2,1)S(1)}, u32[]{:S(2)}, u32[]{:S(2)}) %collective-permute-start.22) | collective-permute-done | bytes 262176 | tf_op jit(solution)/shard_map/ppermute | solution.py:211
  92.9 2.6 %collective-permute-start.28 = (bf16[512,256]{1,0:T(8,128)(2,1)S(1)}, bf16[512,256]{1,0:T(8,128)(2,1)S(1)}, u32[]{:S(2)}, u32[]{:S(2)}) collective-permute-start(bf16[512,256]{1,0:T(8,128)(2,1)S(1)} %get-tuple-element.107), channel_id=1, source_target_pairs={{0,6},{1,7},{2,0},{3,1},{4,2},{5,3},{6,4},{7,5},{8,14},{9,15},{10,... | collective-permute-start | bytes 786440 | tf_op jit(solution)/shard_map/ppermute | solution.py:211
  95.5 5.7 %shard_map.67 = (bf16[512,256]{1,0:T(8,128)(2,1)S(1)}, bf16[512,256]{1,0:T(8,128)(2,1)S(1)}, bf16[512,256]{1,0:T(8,128)(2,1)}, bf16[512,256]{1,0:T(8,128)(2,1)}, bf16[512,256]{1,0:T(8,128)(2,1)S(1)}) custom-call(s32[1]{0:T(128)} %bitcast.2.turn_ref, bf16[256,1024]{1,0:T(8,128)(2,1)S(1)} %collective-permute-done.16.refs_0_, ...), custom_call_target="tpu_custom_call" | custom-call | flops 1 | bytes 1 | tf_op jit(solution)/shard_map/pallas_call | solution.py:184
  101.9 2.4 %collective-permute-done.25.refs_0_ = bf16[256,1024]{1,0:T(8,128)(2,1)S(1)} collective-permute-done((bf16[256,1024]{1,0:T(8,128)(2,1)S(1)}, bf16[256,1024]{1,0:T(8,128)(2,1)S(1)}, u32[]{:S(2)}, u32[]{:S(2)}) %collective-permute-start.25) | collective-permute-done | bytes 524320 | tf_op jit(solution)/shard_map/ppermute | solution.py:315
  108.3 2.7 %collective-permute-start.32 = (bf16[512,256]{1,0:T(8,128)(2,1)}, bf16[512,256]{1,0:T(8,128)(2,1)S(1)}, u32[]{:S(2)}, u32[]{:S(2)}) collective-permute-start(bf16[512,256]{1,0:T(8,128)(2,1)} %get-tuple-element.117), channel_id=1, source_target_pairs={{0,4},{1,5},{2,6},{3,7},{4,0},{5,1},{6,2},{7,3},{8,12},{9,13},{10,... | collective-permute-start | bytes 786440 | tf_op jit(solution)/shard_map/ppermute | solution.py:211
  111.7 4.9 %shard_map.68 = (bf16[512,256]{1,0:T(8,128)(2,1)S(1)}, bf16[512,256]{1,0:T(8,128)(2,1)S(1)}, bf16[512,256]{1,0:T(8,128)(2,1)S(1)}, bf16[512,256]{1,0:T(8,128)(2,1)S(1)}, bf16[512,256]{1,0:T(8,128)(2,1)S(1)}) custom-call(s32[1]{0:T(128)} %bitcast.2.turn_ref, bf16[256,1024]{1,0:T(8,128)(2,1)S(1)} %collective-permute-done.25.refs_0_, ...), custom_call_target="tpu_custom_call" | custom-call | flops 1 | bytes 1 | tf_op jit(solution)/shard_map/pallas_call | solution.py:184
  123.9 4.8 %collective-permute-done.34.refs_7_ = bf16[512,256]{1,0:T(8,128)(2,1)S(1)} collective-permute-done((bf16[512,256]{1,0:T(8,128)(2,1)S(1)}, bf16[512,256]{1,0:T(8,128)(2,1)S(1)}, u32[]{:S(2)}, u32[]{:S(2)}) %collective-permute-start.34) | collective-permute-done | bytes 262176 | tf_op jit(solution)/shard_map/ppermute | solution.py:211
  128.7 5.0 %collective-permute-done.35.refs_8_ = bf16[512,256]{1,0:T(8,128)(2,1)S(1)} collective-permute-done((bf16[512,256]{1,0:T(8,128)(2,1)S(1)}, bf16[512,256]{1,0:T(8,128)(2,1)S(1)}, u32[]{:S(2)}, u32[]{:S(2)}) %collective-permute-start.35) | collective-permute-done | bytes 262176 | tf_op jit(solution)/shard_map/ppermute | solution.py:211
  135.1 3.2 %shard_map.69 = bf16[16,4,32,256]{3,2,1,0:T(8,128)(2,1)} custom-call(s32[1]{0:T(128)} %bitcast.1.y_ref, s32[4,16]{1,0:T(4,128)} %constant_dynamic-slice_fusion.2.sources_ref, bf16[512,256]{1,0:T(8,128)(2,1)} %copy-done.2, bf16[512,256]{1,0:T(8,128)(2,1)} %copy-done.4, bf16[512,256]{1,0:T(8,128)(2,1)} %copy-done.1, bf16[512,256]{1,0:T(8,128)(2,1)} %copy-done.7, ...), custom_call_target="tpu_custom_call" | custom-call | flops 1 | bytes 1 | tf_op jit(solution)/shard_map/pallas_call | solution.py:239
  138.2 4.9 %all-to-all-start = ((bf16[16,4,32,256]{3,2,1,0:T(8,128)(2,1)}), bf16[16,4,32,256]{3,2,1,0:T(8,128)(2,1)S(1)}, u32[]{:S(2)}, u32[]{:S(2)}) async-start(bf16[16,4,32,256]{3,2,1,0:T(8,128)(2,1)} %shard_map.69), calls=%async_computation | async-start | bytes 2097152 | tf_op jit(solution)/shard_map/all_to_all | solution.py:338
  143.1 14.9 %all-to-all-done = bf16[16,4,32,256]{3,2,1,0:T(8,128)(2,1)S(1)} async-done(((bf16[16,4,32,256]{3,2,1,0:T(8,128)(2,1)}), bf16[16,4,32,256]{3,2,1,0:T(8,128)(2,1)S(1)}, u32[]{:S(2)}, u32[]{:S(2)}) %all-to-all-start) | async-done | bytes 1048608 | tf_op jit(solution)/shard_map/all_to_all | solution.py:338
  158.1 3.2 %collective-permute-start.37 = (bf16[4,2,4,32,256]{4,3,2,1,0:T(8,128)(2,1)S(1)}, bf16[4,2,4,32,256]{4,3,2,1,0:T(8,128)(2,1)S(1)}, u32[]{:S(2)}, u32[]{:S(2)}) collective-permute-start(bf16[4,2,4,32,256]{4,3,2,1,0:T(8,128)(2,1)S(1)} %dynamic-slice_bitcast_fusion), channel_id=1, source_target_pairs={{0,1},{1,0},{2,3},{3,2},{4,5},{5,4},{6,7},{7,6},{8,9},{9,8},{10,11... | collective-permute-start | bytes 1572872 | tf_op jit(solution)/shard_map/ppermute | solution.py:312
  (101 shorter events, 48.5 us)
Async XLA Ops:
  2.1 9.9 %collective-permute-start.5 = (bf16[1024,256]{1,0:T(8,128)(2,1)S(1)}, bf16[1024,256]{1,0:T(8,128)(2,1)}, u32[]{:S(2)}, u32[]{:S(2)}) collective-permute-start(bf16[1024,256]{1,0:T(8,128)(2,1)S(1)} %get-tuple-element.131), channel_id=1, source_target_pairs={{0,1},{1,0},{2,3},{3,2},{4,5},{5,4},{6,7},{7,6},{8,9},{9,8},{10,11... | collective-permute-start | bytes 1572872 | tf_op jit(solution)/shard_map/ppermute | solution.py:300
  5.2 24.2 %collective-permute-start.4 = (bf16[1024,256]{1,0:T(8,128)(2,1)}, bf16[1024,256]{1,0:T(8,128)(2,1)}, u32[]{:S(2)}, u32[]{:S(2)}) collective-permute-start(bf16[1024,256]{1,0:T(8,128)(2,1)} %get-tuple-element.79.refs_4_), channel_id=1, source_target_pairs={{0,96},{8,104},{16,112},{24,120},{32,0},{40,8},{48,16},{56,24},{64... | collective-permute-start | bytes 1572872 | tf_op jit(solution)/shard_map/ppermute | solution.py:301
  12.0 17.3 %collective-permute-start.6 = (bf16[1024,256]{1,0:T(8,128)(2,1)}, bf16[1024,256]{1,0:T(8,128)(2,1)}, u32[]{:S(2)}, u32[]{:S(2)}) collective-permute-start(bf16[1024,256]{1,0:T(8,128)(2,1)} %collective-permute-done.5.refs_5_), channel_id=1, source_target_pairs={{0,32},{8,40},{16,48},{24,56},{32,64},{40,72},{48,80},{56,88},{64,... | collective-permute-start | bytes 1572872 | tf_op jit(solution)/shard_map/ppermute | solution.py:302
  14.4 13.1 %collective-permute-start.2 = (bf16[512,256]{1,0:T(8,128)(2,1)S(1)}, bf16[512,256]{1,0:T(8,128)(2,1)}, u32[]{:S(2)}, u32[]{:S(2)}) collective-permute-start(bf16[512,256]{1,0:T(8,128)(2,1)S(1)} %get-tuple-element.134), channel_id=1, source_target_pairs={{0,16},{8,24},{16,0},{24,8},{32,48},{40,56},{48,32},{56,40},{64,80... | collective-permute-start | bytes 786440 | tf_op jit(solution)/shard_map/ppermute | solution.py:293
  17.0 12.4 %collective-permute-start.3 = (bf16[512,256]{1,0:T(8,128)(2,1)S(1)}, bf16[512,256]{1,0:T(8,128)(2,1)}, u32[]{:S(2)}, u32[]{:S(2)}) collective-permute-start(bf16[512,256]{1,0:T(8,128)(2,1)S(1)} %get-tuple-element.133), channel_id=1, source_target_pairs={{0,24},{8,0},{16,8},{24,16},{32,56},{40,32},{48,40},{56,48},{64,88... | collective-permute-start | bytes 786440 | tf_op jit(solution)/shard_map/ppermute | solution.py:293
  20.9 18.2 %collective-permute-start.10 = (bf16[1024,256]{1,0:T(8,128)(2,1)}, bf16[1024,256]{1,0:T(8,128)(2,1)}, u32[]{:S(2)}, u32[]{:S(2)}) collective-permute-start(bf16[1024,256]{1,0:T(8,128)(2,1)} %get-tuple-element.79.refs_4_), channel_id=1, source_target_pairs={{0,32},{8,40},{16,48},{24,56},{32,64},{40,72},{48,80},{56,88},{64,... | collective-permute-start | bytes 1572872 | tf_op jit(solution)/shard_map/ppermute | solution.py:303
  27.5 11.6 %collective-permute-start.7 = (bf16[1024,256]{1,0:T(8,128)(2,1)}, bf16[1024,256]{1,0:T(8,128)(2,1)}, u32[]{:S(2)}, u32[]{:S(2)}) collective-permute-start(bf16[1024,256]{1,0:T(8,128)(2,1)} %collective-permute-done.5.refs_5_), channel_id=1, source_target_pairs={{0,96},{8,104},{16,112},{24,120},{32,0},{40,8},{48,16},{56,24},{64... | collective-permute-start | bytes 1572872 | tf_op jit(solution)/shard_map/ppermute | solution.py:301
  29.4 20.6 %collective-permute-start.8 = (bf16[1024,256]{1,0:T(8,128)(2,1)}, bf16[1024,256]{1,0:T(8,128)(2,1)}, u32[]{:S(2)}, u32[]{:S(2)}) collective-permute-start(bf16[1024,256]{1,0:T(8,128)(2,1)} %collective-permute-done.4.refs_6_), channel_id=1, source_target_pairs={{0,96},{8,104},{16,112},{24,120},{32,0},{40,8},{48,16},{56,24},{64... | collective-permute-start | bytes 1572872 | tf_op jit(solution)/shard_map/ppermute | solution.py:305
  29.7 20.3 %collective-permute-start.9 = (bf16[1024,256]{1,0:T(8,128)(2,1)}, bf16[1024,256]{1,0:T(8,128)(2,1)}, u32[]{:S(2)}, u32[]{:S(2)}) collective-permute-start(bf16[1024,256]{1,0:T(8,128)(2,1)} %collective-permute-done.6.refs_11_), channel_id=1, source_target_pairs={{0,32},{8,40},{16,48},{24,56},{32,64},{40,72},{48,80},{56,88},{64,... | collective-permute-start | bytes 1572872 | tf_op jit(solution)/shard_map/ppermute | solution.py:306
  53.4 13.2 %collective-permute-start.11 = (bf16[256,1024]{1,0:T(8,128)(2,1)}, bf16[256,1024]{1,0:T(8,128)(2,1)S(1)}, u32[]{:S(2)}, u32[]{:S(2)}) collective-permute-start(bf16[256,1024]{1,0:T(8,128)(2,1)} %get-tuple-element.90.refs_0_), channel_id=1, source_target_pairs={{0,24},{8,0},{16,8},{24,16},{32,56},{40,32},{48,40},{56,48},{64,88... | collective-permute-start | bytes 1572872 | tf_op jit(solution)/shard_map/ppermute | solution.py:315
  53.4 14.1 %collective-permute-start.12 = (bf16[256,1024]{1,0:T(8,128)(2,1)}, bf16[256,1024]{1,0:T(8,128)(2,1)S(1)}, u32[]{:S(2)}, u32[]{:S(2)}) collective-permute-start(bf16[256,1024]{1,0:T(8,128)(2,1)} %get-tuple-element.89.refs_1_), channel_id=1, source_target_pairs={{0,8},{8,16},{16,24},{24,0},{32,40},{40,48},{48,56},{56,32},{64,72... | collective-permute-start | bytes 1572872 | tf_op jit(solution)/shard_map/ppermute | solution.py:315
  60.8 10.0 %collective-permute-start.15 = (bf16[512,256]{1,0:T(8,128)(2,1)S(1)}, bf16[512,256]{1,0:T(8,128)(2,1)S(1)}, u32[]{:S(2)}, u32[]{:S(2)}) collective-permute-start(bf16[512,256]{1,0:T(8,128)(2,1)S(1)} %get-tuple-element.88), channel_id=1, source_target_pairs={{0,4},{1,5},{2,6},{3,7},{4,0},{5,1},{6,2},{7,3},{8,12},{9,13},{10,... | collective-permute-start | bytes 786440 | tf_op jit(solution)/shard_map/ppermute | solution.py:211
  71.7 13.2 %collective-permute-start.16 = (bf16[256,1024]{1,0:T(8,128)(2,1)}, bf16[256,1024]{1,0:T(8,128)(2,1)S(1)}, u32[]{:S(2)}, u32[]{:S(2)}) collective-permute-start(bf16[256,1024]{1,0:T(8,128)(2,1)} %get-tuple-element.89.refs_1_), channel_id=1, source_target_pairs={{0,24},{8,0},{16,8},{24,16},{32,56},{40,32},{48,40},{56,48},{64,88... | collective-permute-start | bytes 1572872 | tf_op jit(solution)/shard_map/ppermute | solution.py:315
  72.0 14.1 %collective-permute-start.17 = (bf16[256,1024]{1,0:T(8,128)(2,1)}, bf16[256,1024]{1,0:T(8,128)(2,1)S(1)}, u32[]{:S(2)}, u32[]{:S(2)}) collective-permute-start(bf16[256,1024]{1,0:T(8,128)(2,1)} %get-tuple-element.90.refs_0_), channel_id=1, source_target_pairs={{0,8},{8,16},{16,24},{24,0},{32,40},{40,48},{48,56},{56,32},{64,72... | collective-permute-start | bytes 1572872 | tf_op jit(solution)/shard_map/ppermute | solution.py:315
  73.2 9.1 %collective-permute-start.18 = (bf16[512,256]{1,0:T(8,128)(2,1)S(1)}, bf16[512,256]{1,0:T(8,128)(2,1)S(1)}, u32[]{:S(2)}, u32[]{:S(2)}) collective-permute-start(bf16[512,256]{1,0:T(8,128)(2,1)S(1)} %get-tuple-element.93), channel_id=1, source_target_pairs={{0,2},{1,3},{2,4},{3,5},{4,6},{5,7},{6,0},{7,1},{8,10},{9,11},{10,... | collective-permute-start | bytes 786440 | tf_op jit(solution)/shard_map/ppermute | solution.py:211
  91.3 13.0 %collective-permute-start.25 = (bf16[256,1024]{1,0:T(8,128)(2,1)S(1)}, bf16[256,1024]{1,0:T(8,128)(2,1)S(1)}, u32[]{:S(2)}, u32[]{:S(2)}) collective-permute-start(bf16[256,1024]{1,0:T(8,128)(2,1)S(1)} %collective-permute-done.11.refs_0_), channel_id=1, source_target_pairs={{0,24},{8,0},{16,8},{24,16},{32,56},{40,32},{48,40},{56,48},{64,88... | collective-permute-start | bytes 1572872 | tf_op jit(solution)/shard_map/ppermute | solution.py:315
  92.7 13.9 %collective-permute-start.26 = (bf16[256,1024]{1,0:T(8,128)(2,1)S(1)}, bf16[256,1024]{1,0:T(8,128)(2,1)S(1)}, u32[]{:S(2)}, u32[]{:S(2)}) collective-permute-start(bf16[256,1024]{1,0:T(8,128)(2,1)S(1)} %collective-permute-done.12.refs_1_), channel_id=1, source_target_pairs={{0,8},{8,16},{16,24},{24,0},{32,40},{40,48},{48,56},{56,32},{64,72... | collective-permute-start | bytes 1572872 | tf_op jit(solution)/shard_map/ppermute | solution.py:315
  108.3 11.4 %collective-permute-start.31 = (bf16[512,256]{1,0:T(8,128)(2,1)S(1)}, bf16[512,256]{1,0:T(8,128)(2,1)S(1)}, u32[]{:S(2)}, u32[]{:S(2)}) collective-permute-start(bf16[512,256]{1,0:T(8,128)(2,1)S(1)} %get-tuple-element.116), channel_id=1, source_target_pairs={{0,2},{1,3},{2,4},{3,5},{4,6},{5,7},{6,0},{7,1},{8,10},{9,11},{10,... | collective-permute-start | bytes 786440 | tf_op jit(solution)/shard_map/ppermute | solution.py:211
  108.3 14.2 %collective-permute-start.32 = (bf16[512,256]{1,0:T(8,128)(2,1)}, bf16[512,256]{1,0:T(8,128)(2,1)S(1)}, u32[]{:S(2)}, u32[]{:S(2)}) collective-permute-start(bf16[512,256]{1,0:T(8,128)(2,1)} %get-tuple-element.117), channel_id=1, source_target_pairs={{0,4},{1,5},{2,6},{3,7},{4,0},{5,1},{6,2},{7,3},{8,12},{9,13},{10,... | collective-permute-start | bytes 786440 | tf_op jit(solution)/shard_map/ppermute | solution.py:211
  111.0 12.9 %collective-permute-start.33 = (bf16[512,256]{1,0:T(8,128)(2,1)}, bf16[512,256]{1,0:T(8,128)(2,1)S(1)}, u32[]{:S(2)}, u32[]{:S(2)}) collective-permute-start(bf16[512,256]{1,0:T(8,128)(2,1)} %get-tuple-element.118), channel_id=1, source_target_pairs={{0,6},{1,7},{2,0},{3,1},{4,2},{5,3},{6,4},{7,5},{8,14},{9,15},{10,... | collective-permute-start | bytes 786440 | tf_op jit(solution)/shard_map/ppermute | solution.py:211
  118.0 10.7 %collective-permute-start.34 = (bf16[512,256]{1,0:T(8,128)(2,1)S(1)}, bf16[512,256]{1,0:T(8,128)(2,1)S(1)}, u32[]{:S(2)}, u32[]{:S(2)}) collective-permute-start(bf16[512,256]{1,0:T(8,128)(2,1)S(1)} %get-tuple-element.120), channel_id=1, source_target_pairs={{0,2},{1,3},{2,4},{3,5},{4,6},{5,7},{6,0},{7,1},{8,10},{9,11},{10,... | collective-permute-start | bytes 786440 | tf_op jit(solution)/shard_map/ppermute | solution.py:211
  118.7 15.0 %collective-permute-start.35 = (bf16[512,256]{1,0:T(8,128)(2,1)S(1)}, bf16[512,256]{1,0:T(8,128)(2,1)S(1)}, u32[]{:S(2)}, u32[]{:S(2)}) collective-permute-start(bf16[512,256]{1,0:T(8,128)(2,1)S(1)} %get-tuple-element.121), channel_id=1, source_target_pairs={{0,4},{1,5},{2,6},{3,7},{4,0},{5,1},{6,2},{7,3},{8,12},{9,13},{10,... | collective-permute-start | bytes 786440 | tf_op jit(solution)/shard_map/ppermute | solution.py:211
  119.7 14.7 %collective-permute-start.36 = (bf16[512,256]{1,0:T(8,128)(2,1)S(1)}, bf16[512,256]{1,0:T(8,128)(2,1)S(1)}, u32[]{:S(2)}, u32[]{:S(2)}) collective-permute-start(bf16[512,256]{1,0:T(8,128)(2,1)S(1)} %get-tuple-element.122), channel_id=1, source_target_pairs={{0,6},{1,7},{2,0},{3,1},{4,2},{5,3},{6,4},{7,5},{8,14},{9,15},{10,... | collective-permute-start | bytes 786440 | tf_op jit(solution)/shard_map/ppermute | solution.py:211
  138.2 19.8 %all-to-all-start = ((bf16[16,4,32,256]{3,2,1,0:T(8,128)(2,1)}), bf16[16,4,32,256]{3,2,1,0:T(8,128)(2,1)S(1)}, u32[]{:S(2)}, u32[]{:S(2)}) async-start(bf16[16,4,32,256]{3,2,1,0:T(8,128)(2,1)} %shard_map.69), calls=%async_computation | async-start | bytes 2097152 | tf_op jit(solution)/shard_map/all_to_all | solution.py:338
  (31 other events, 303.4 us)

commit v2 on v1

--- a/solution.py
+++ b/solution.py
@@ -330,7 +330,7 @@
     inner, outer, own, _ = meet(inner, outer, own, outer_terms[:1] + outer_terms[2:3])
     far = [along(outer[0], 1), along(outer[1], 3)]
     inner_terms, own = terms(inner, finished=own)
-    far, outer_terms, _ = meet(far, outer_terms, inner_terms[:1])
+    far, _ = meet(far, inner_terms[:1] + outer_terms[1:2])
     far_terms, outer = terms(far, finished=outer_terms)
     inner_terms, far_terms = meet(inner_terms, far_terms)
     sources = lax.dynamic_slice_in_dim(assignment, x * SIDE, SIDE, axis=0)

time: 164 us -> 167 us (1.018)
  starting transfers between devices: 52.4 us -> 56.9 us
    ppermute x9, starting transfers between devices: 11.4 us -> 17.6 us  [swap(): return lax.ppermute(a, 'tp', CORES)]
    all_to_all x1, waiting for transfers between devices: 14.9 us -> 11.7 us  [shards(): lax.all_to_all(outgoing, 'ctx', split_axis=0, concat_axis=0, tiled=True)]
where the time goes in v2:
time: 167 us
  waiting for transfers between devices  71.3 us (43%)
  starting transfers between devices  56.9 us (34%)
  Pallas kernels  31.8 us (19%)
  local copies, waits for them, and re-layouts  5.87 us (4%)
    pallas_call x4, Pallas kernels, project(): pl.pallas_call(functools.partial(project_kernel, count), in_specs=[pl.Blo...  20 us
    ppermute x12, waiting for transfers between devices, spread_z(): lax.ppermute(pieces[e], 'tp', z_shift(e))  18.2 us
    ppermute x9, starting transfers between devices, swap(): return lax.ppermute(a, 'tp', CORES)  17.6 us
    ppermute x12, starting transfers between devices, spread_z(): lax.ppermute(pieces[e], 'tp', z_shift(e))  16.7 us
    ppermute x6, waiting for transfers between devices, along(): return lax.ppermute(a, 'ctx', grid_shift(0, -steps))  12.6 us
    all_to_all x1, waiting for transfers between devices, shards(): lax.all_to_all(outgoing, 'ctx', split_axis=0, concat_axis=0, tiled=True)  11.7 us
    ppermute x1, waiting for transfers between devices, shards(): kept_far = lax.ppermute(kept_next, 'ctx', grid_shift(-1, 0))  10.7 us
    ppermute x3, waiting for transfers between devices, shards(): lax.ppermute(jnp.where(y + k < SIDE, both, above), 'ctx', grid_shift(0, k))  9.03 us
  transfers between devices with their start and end apart: 39, of which 22 were waited for; matrix products, arithmetic and copies ran while one was open for 1% of the time, Pallas kernels for 17%

profile of v2, /device:TPU:1, one launch (start us, length us, event | category | flops | bytes accessed | tf_op | source)
XLA Modules:
  0.0 166.8 jit_solution(12160773933070201598)
XLA Ops:
  6.5 5.5 %collective-permute-done.rest_0_ = bf16[512,256]{1,0:T(8,128)(2,1)S(1)} collective-permute-done((bf16[512,256]{1,0:T(8,128)(2,1)S(1)}, bf16[512,256]{1,0:T(8,128)(2,1)S(1)}, u32[]{:S(2)}, u32[]{:S(2)}) %collective-permute-start) | collective-permute-done | bytes 262176 | tf_op jit(solution)/shard_map/ppermute | solution.py:291
  14.4 2.6 %collective-permute-start.2 = (bf16[512,256]{1,0:T(8,128)(2,1)S(1)}, bf16[512,256]{1,0:T(8,128)(2,1)}, u32[]{:S(2)}, u32[]{:S(2)}) collective-permute-start(bf16[512,256]{1,0:T(8,128)(2,1)S(1)} %get-tuple-element.126), channel_id=1, source_target_pairs={{0,16},{8,24},{16,0},{24,8},{32,48},{40,56},{48,32},{56,40},{64,80... | collective-permute-start | bytes 786440 | tf_op jit(solution)/shard_map/ppermute | solution.py:293
  18.1 2.9 %collective-permute-done.1.rest_3_ = bf16[512,256]{1,0:T(8,128)(2,1)} collective-permute-done((bf16[512,256]{1,0:T(8,128)(2,1)S(1)}, bf16[512,256]{1,0:T(8,128)(2,1)}, u32[]{:S(2)}, u32[]{:S(2)}) %collective-permute-start.1) | collective-permute-done | bytes 262176 | tf_op jit(solution)/shard_map/ppermute | solution.py:293
  21.4 6.1 %collective-permute-done.2.rest_2_ = bf16[512,256]{1,0:T(8,128)(2,1)} collective-permute-done((bf16[512,256]{1,0:T(8,128)(2,1)S(1)}, bf16[512,256]{1,0:T(8,128)(2,1)}, u32[]{:S(2)}, u32[]{:S(2)}) %collective-permute-start.2) | collective-permute-done | bytes 262176 | tf_op jit(solution)/shard_map/ppermute | solution.py:293
  31.7 7.6 %shard_map.64 = (bf16[256,1024]{1,0:T(8,128)(2,1)}, bf16[256,1024]{1,0:T(8,128)(2,1)}) custom-call(s32[8]{0:T(128)} %broadcast_subtract_fusion.firsts_ref, bf16[512,1024]{1,0:T(8,128)(2,1)} %q_ref.1, bf16[512,256]{1,0:T(8,128)(2,1)} %copy-done.6, bf16[512,256]{1,0:T(8,128)(2,1)} %collective-permute-done.3.rest_1_, ...), custom_call_target="tpu_custom_call" | custom-call | flops 1 | bytes 1 | tf_op jit(solution)/shard_map/pallas_call | solution.py:121
  39.2 10.7 %collective-permute-done.8.refs_8_ = bf16[1024,256]{1,0:T(8,128)(2,1)} collective-permute-done((bf16[1024,256]{1,0:T(8,128)(2,1)}, bf16[1024,256]{1,0:T(8,128)(2,1)}, u32[]{:S(2)}, u32[]{:S(2)}) %collective-permute-start.8) | collective-permute-done | bytes 524320 | tf_op jit(solution)/shard_map/ppermute | solution.py:305
  50.0 3.4 %collective-permute-start.13 = (bf16[256,1024]{1,0:T(8,128)(2,1)}, bf16[256,1024]{1,0:T(8,128)(2,1)S(1)}, u32[]{:S(2)}, u32[]{:S(2)}) collective-permute-start(bf16[256,1024]{1,0:T(8,128)(2,1)} %get-tuple-element.86.refs_0_), channel_id=1, source_target_pairs={{0,1},{1,0},{2,3},{3,2},{4,5},{5,4},{6,7},{7,6},{8,9},{9,8},{10,11... | collective-permute-start | bytes 1572872 | tf_op jit(solution)/shard_map/ppermute | solution.py:312
  55.9 4.9 %shard_map.65 = (bf16[512,256]{1,0:T(8,128)(2,1)S(1)}, bf16[512,256]{1,0:T(8,128)(2,1)S(1)}, bf16[512,256]{1,0:T(8,128)(2,1)S(1)}, bf16[512,256]{1,0:T(8,128)(2,1)S(1)}) custom-call(s32[1]{0:T(128)} %bitcast.2.turn_ref, bf16[256,1024]{1,0:T(8,128)(2,1)} %get-tuple-element.86.refs_0_, bf16[256,1024]{1,0:T(8,128)(2,1)} %get-tuple-element.85.refs_1_, ...), custom_call_target="tpu_custom_call" | custom-call | flops 1 | bytes 1 | tf_op jit(solution)/shard_map/pallas_call | solution.py:184
  60.8 3.7 %collective-permute-start.15 = (bf16[512,256]{1,0:T(8,128)(2,1)S(1)}, bf16[512,256]{1,0:T(8,128)(2,1)S(1)}, u32[]{:S(2)}, u32[]{:S(2)}) collective-permute-start(bf16[512,256]{1,0:T(8,128)(2,1)S(1)} %get-tuple-element.84), channel_id=1, source_target_pairs={{0,4},{1,5},{2,6},{3,7},{4,0},{5,1},{6,2},{7,3},{8,12},{9,13},{10,... | collective-permute-start | bytes 786440 | tf_op jit(solution)/shard_map/ppermute | solution.py:211
  67.5 3.3 %collective-permute-done.15.refs_14_ = bf16[512,256]{1,0:T(8,128)(2,1)S(1)} collective-permute-done((bf16[512,256]{1,0:T(8,128)(2,1)S(1)}, bf16[512,256]{1,0:T(8,128)(2,1)S(1)}, u32[]{:S(2)}, u32[]{:S(2)}) %collective-permute-start.15) | collective-permute-done | bytes 262176 | tf_op jit(solution)/shard_map/ppermute | solution.py:211
  76.4 4.6 %shard_map.66 = (bf16[512,256]{1,0:T(8,128)(2,1)S(1)}, bf16[512,256]{1,0:T(8,128)(2,1)S(1)}, bf16[512,256]{1,0:T(8,128)(2,1)S(1)}, bf16[512,256]{1,0:T(8,128)(2,1)S(1)}) custom-call(s32[1]{0:T(128)} %bitcast.2.turn_ref, bf16[256,1024]{1,0:T(8,128)(2,1)S(1)} %collective-permute-done.11.refs_0_, bf16[256,1024]{1,0:T(8,128)(2,1)S(1)} %collective-permute-done.12.refs_1_, ...), custom_call_target="tpu_custom_call" | custom-call | flops 1 | bytes 1 | tf_op jit(solution)/shard_map/pallas_call | solution.py:184
  82.4 2.6 %collective-permute-done.16.refs_0_ = bf16[256,1024]{1,0:T(8,128)(2,1)S(1)} collective-permute-done((bf16[256,1024]{1,0:T(8,128)(2,1)}, bf16[256,1024]{1,0:T(8,128)(2,1)S(1)}, u32[]{:S(2)}, u32[]{:S(2)}) %collective-permute-start.16) | collective-permute-done | bytes 524320 | tf_op jit(solution)/shard_map/ppermute | solution.py:315
  86.1 3.1 %collective-permute-done.22.refs_14_ = bf16[512,256]{1,0:T(8,128)(2,1)S(1)} collective-permute-done((bf16[512,256]{1,0:T(8,128)(2,1)S(1)}, bf16[512,256]{1,0:T(8,128)(2,1)S(1)}, u32[]{:S(2)}, u32[]{:S(2)}) %collective-permute-start.22) | collective-permute-done | bytes 262176 | tf_op jit(solution)/shard_map/ppermute | solution.py:211
  93.6 5.7 %shard_map.67 = (bf16[512,256]{1,0:T(8,128)(2,1)S(1)}, bf16[512,256]{1,0:T(8,128)(2,1)S(1)}, bf16[512,256]{1,0:T(8,128)(2,1)}, bf16[512,256]{1,0:T(8,128)(2,1)}, bf16[512,256]{1,0:T(8,128)(2,1)S(1)}) custom-call(s32[1]{0:T(128)} %bitcast.2.turn_ref, bf16[256,1024]{1,0:T(8,128)(2,1)S(1)} %collective-permute-done.16.refs_0_, ...), custom_call_target="tpu_custom_call" | custom-call | flops 1 | bytes 1 | tf_op jit(solution)/shard_map/pallas_call | solution.py:184
  100.8 3.6 %collective-permute-done.25.refs_0_ = bf16[256,1024]{1,0:T(8,128)(2,1)S(1)} collective-permute-done((bf16[256,1024]{1,0:T(8,128)(2,1)S(1)}, bf16[256,1024]{1,0:T(8,128)(2,1)S(1)}, u32[]{:S(2)}, u32[]{:S(2)}) %collective-permute-start.25) | collective-permute-done | bytes 524320 | tf_op jit(solution)/shard_map/ppermute | solution.py:315
  104.3 2.3 %collective-permute-done.26.refs_1_ = bf16[256,1024]{1,0:T(8,128)(2,1)S(1)} collective-permute-done((bf16[256,1024]{1,0:T(8,128)(2,1)S(1)}, bf16[256,1024]{1,0:T(8,128)(2,1)S(1)}, u32[]{:S(2)}, u32[]{:S(2)}) %collective-permute-start.26) | collective-permute-done | bytes 524320 | tf_op jit(solution)/shard_map/ppermute | solution.py:315
  111.1 4.6 %collective-permute-done.30.refs_15_ = bf16[512,256]{1,0:T(8,128)(2,1)S(1)} collective-permute-done((bf16[512,256]{1,0:T(8,128)(2,1)S(1)}, bf16[512,256]{1,0:T(8,128)(2,1)S(1)}, u32[]{:S(2)}, u32[]{:S(2)}) %collective-permute-start.30) | collective-permute-done | bytes 262176 | tf_op jit(solution)/shard_map/ppermute | solution.py:211
  115.7 3.0 %collective-permute-start.33 = (bf16[512,256]{1,0:T(8,128)(2,1)}, bf16[512,256]{1,0:T(8,128)(2,1)S(1)}, u32[]{:S(2)}, u32[]{:S(2)}) collective-permute-start(bf16[512,256]{1,0:T(8,128)(2,1)} %get-tuple-element.110), channel_id=1, source_target_pairs={{0,6},{1,7},{2,0},{3,1},{4,2},{5,3},{6,4},{7,5},{8,14},{9,15},{10,... | collective-permute-start | bytes 786440 | tf_op jit(solution)/shard_map/ppermute | solution.py:211
  118.6 4.9 %shard_map.68 = (bf16[512,256]{1,0:T(8,128)(2,1)S(1)}, bf16[512,256]{1,0:T(8,128)(2,1)S(1)}, bf16[512,256]{1,0:T(8,128)(2,1)S(1)}, bf16[512,256]{1,0:T(8,128)(2,1)S(1)}, bf16[512,256]{1,0:T(8,128)(2,1)S(1)}) custom-call(s32[1]{0:T(128)} %bitcast.2.turn_ref, bf16[256,1024]{1,0:T(8,128)(2,1)S(1)} %collective-permute-done.25.refs_0_, ...), custom_call_target="tpu_custom_call" | custom-call | flops 1 | bytes 1 | tf_op jit(solution)/shard_map/pallas_call | solution.py:184
  128.3 5.9 %collective-permute-done.34.refs_7_ = bf16[512,256]{1,0:T(8,128)(2,1)S(1)} collective-permute-done((bf16[512,256]{1,0:T(8,128)(2,1)S(1)}, bf16[512,256]{1,0:T(8,128)(2,1)S(1)}, u32[]{:S(2)}, u32[]{:S(2)}) %collective-permute-start.34) | collective-permute-done | bytes 262176 | tf_op jit(solution)/shard_map/ppermute | solution.py:211
  135.5 3.2 %shard_map.69 = bf16[16,4,32,256]{3,2,1,0:T(8,128)(2,1)} custom-call(s32[1]{0:T(128)} %bitcast.1.y_ref, s32[4,16]{1,0:T(4,128)} %constant_dynamic-slice_fusion.2.sources_ref, bf16[512,256]{1,0:T(8,128)(2,1)} %copy-done.2, bf16[512,256]{1,0:T(8,128)(2,1)} %copy-done.4, bf16[512,256]{1,0:T(8,128)(2,1)} %copy-done.1, bf16[512,256]{1,0:T(8,128)(2,1)} %copy-done.7, ...), custom_call_target="tpu_custom_call" | custom-call | flops 1 | bytes 1 | tf_op jit(solution)/shard_map/pallas_call | solution.py:239
  138.7 4.3 %all-to-all-start = ((bf16[16,4,32,256]{3,2,1,0:T(8,128)(2,1)}), bf16[16,4,32,256]{3,2,1,0:T(8,128)(2,1)S(1)}, u32[]{:S(2)}, u32[]{:S(2)}) async-start(bf16[16,4,32,256]{3,2,1,0:T(8,128)(2,1)} %shard_map.69), calls=%async_computation | async-start | bytes 2097152 | tf_op jit(solution)/shard_map/all_to_all | solution.py:338
  143.1 11.7 %all-to-all-done = bf16[16,4,32,256]{3,2,1,0:T(8,128)(2,1)S(1)} async-done(((bf16[16,4,32,256]{3,2,1,0:T(8,128)(2,1)}), bf16[16,4,32,256]{3,2,1,0:T(8,128)(2,1)S(1)}, u32[]{:S(2)}, u32[]{:S(2)}) %all-to-all-start) | async-done | bytes 1048608 | tf_op jit(solution)/shard_map/all_to_all | solution.py:338
  154.8 9.4 %collective-permute-start.37 = (bf16[4,2,4,32,256]{4,3,2,1,0:T(8,128)(2,1)S(1)}, bf16[4,2,4,32,256]{4,3,2,1,0:T(8,128)(2,1)S(1)}, u32[]{:S(2)}, u32[]{:S(2)}) collective-permute-start(bf16[4,2,4,32,256]{4,3,2,1,0:T(8,128)(2,1)S(1)} %dynamic-slice_bitcast_fusion), channel_id=1, source_target_pairs={{0,1},{1,0},{2,3},{3,2},{4,5},{5,4},{6,7},{7,6},{8,9},{9,8},{10,11... | collective-permute-start | bytes 1572872 | tf_op jit(solution)/shard_map/ppermute | solution.py:312
  (101 shorter events, 47.1 us)
Async XLA Ops:
  2.1 9.9 %collective-permute-start.5 = (bf16[1024,256]{1,0:T(8,128)(2,1)S(1)}, bf16[1024,256]{1,0:T(8,128)(2,1)}, u32[]{:S(2)}, u32[]{:S(2)}) collective-permute-start(bf16[1024,256]{1,0:T(8,128)(2,1)S(1)} %get-tuple-element.123), channel_id=1, source_target_pairs={{0,1},{1,0},{2,3},{3,2},{4,5},{5,4},{6,7},{7,6},{8,9},{9,8},{10,11... | collective-permute-start | bytes 1572872 | tf_op jit(solution)/shard_map/ppermute | solution.py:300
  5.2 24.2 %collective-permute-start.4 = (bf16[1024,256]{1,0:T(8,128)(2,1)}, bf16[1024,256]{1,0:T(8,128)(2,1)}, u32[]{:S(2)}, u32[]{:S(2)}) collective-permute-start(bf16[1024,256]{1,0:T(8,128)(2,1)} %get-tuple-element.75.refs_4_), channel_id=1, source_target_pairs={{0,96},{8,104},{16,112},{24,120},{32,0},{40,8},{48,16},{56,24},{64... | collective-permute-start | bytes 1572872 | tf_op jit(solution)/shard_map/ppermute | solution.py:301
  12.0 17.3 %collective-permute-start.6 = (bf16[1024,256]{1,0:T(8,128)(2,1)}, bf16[1024,256]{1,0:T(8,128)(2,1)}, u32[]{:S(2)}, u32[]{:S(2)}) collective-permute-start(bf16[1024,256]{1,0:T(8,128)(2,1)} %collective-permute-done.5.refs_5_), channel_id=1, source_target_pairs={{0,32},{8,40},{16,48},{24,56},{32,64},{40,72},{48,80},{56,88},{64,... | collective-permute-start | bytes 1572872 | tf_op jit(solution)/shard_map/ppermute | solution.py:302
  14.4 13.1 %collective-permute-start.2 = (bf16[512,256]{1,0:T(8,128)(2,1)S(1)}, bf16[512,256]{1,0:T(8,128)(2,1)}, u32[]{:S(2)}, u32[]{:S(2)}) collective-permute-start(bf16[512,256]{1,0:T(8,128)(2,1)S(1)} %get-tuple-element.126), channel_id=1, source_target_pairs={{0,16},{8,24},{16,0},{24,8},{32,48},{40,56},{48,32},{56,40},{64,80... | collective-permute-start | bytes 786440 | tf_op jit(solution)/shard_map/ppermute | solution.py:293
  17.0 12.4 %collective-permute-start.3 = (bf16[512,256]{1,0:T(8,128)(2,1)S(1)}, bf16[512,256]{1,0:T(8,128)(2,1)}, u32[]{:S(2)}, u32[]{:S(2)}) collective-permute-start(bf16[512,256]{1,0:T(8,128)(2,1)S(1)} %get-tuple-element.125), channel_id=1, source_target_pairs={{0,24},{8,0},{16,8},{24,16},{32,56},{40,32},{48,40},{56,48},{64,88... | collective-permute-start | bytes 786440 | tf_op jit(solution)/shard_map/ppermute | solution.py:293
  20.9 18.3 %collective-permute-start.10 = (bf16[1024,256]{1,0:T(8,128)(2,1)}, bf16[1024,256]{1,0:T(8,128)(2,1)}, u32[]{:S(2)}, u32[]{:S(2)}) collective-permute-start(bf16[1024,256]{1,0:T(8,128)(2,1)} %get-tuple-element.75.refs_4_), channel_id=1, source_target_pairs={{0,32},{8,40},{16,48},{24,56},{32,64},{40,72},{48,80},{56,88},{64,... | collective-permute-start | bytes 1572872 | tf_op jit(solution)/shard_map/ppermute | solution.py:303
  27.5 11.7 %collective-permute-start.7 = (bf16[1024,256]{1,0:T(8,128)(2,1)}, bf16[1024,256]{1,0:T(8,128)(2,1)}, u32[]{:S(2)}, u32[]{:S(2)}) collective-permute-start(bf16[1024,256]{1,0:T(8,128)(2,1)} %collective-permute-done.5.refs_5_), channel_id=1, source_target_pairs={{0,96},{8,104},{16,112},{24,120},{32,0},{40,8},{48,16},{56,24},{64... | collective-permute-start | bytes 1572872 | tf_op jit(solution)/shard_map/ppermute | solution.py:301
  29.4 20.6 %collective-permute-start.8 = (bf16[1024,256]{1,0:T(8,128)(2,1)}, bf16[1024,256]{1,0:T(8,128)(2,1)}, u32[]{:S(2)}, u32[]{:S(2)}) collective-permute-start(bf16[1024,256]{1,0:T(8,128)(2,1)} %collective-permute-done.4.refs_6_), channel_id=1, source_target_pairs={{0,96},{8,104},{16,112},{24,120},{32,0},{40,8},{48,16},{56,24},{64... | collective-permute-start | bytes 1572872 | tf_op jit(solution)/shard_map/ppermute | solution.py:305
  29.7 20.3 %collective-permute-start.9 = (bf16[1024,256]{1,0:T(8,128)(2,1)}, bf16[1024,256]{1,0:T(8,128)(2,1)}, u32[]{:S(2)}, u32[]{:S(2)}) collective-permute-start(bf16[1024,256]{1,0:T(8,128)(2,1)} %collective-permute-done.6.refs_11_), channel_id=1, source_target_pairs={{0,32},{8,40},{16,48},{24,56},{32,64},{40,72},{48,80},{56,88},{64,... | collective-permute-start | bytes 1572872 | tf_op jit(solution)/shard_map/ppermute | solution.py:306
  53.4 13.2 %collective-permute-start.11 = (bf16[256,1024]{1,0:T(8,128)(2,1)}, bf16[256,1024]{1,0:T(8,128)(2,1)S(1)}, u32[]{:S(2)}, u32[]{:S(2)}) collective-permute-start(bf16[256,1024]{1,0:T(8,128)(2,1)} %get-tuple-element.86.refs_0_), channel_id=1, source_target_pairs={{0,24},{8,0},{16,8},{24,16},{32,56},{40,32},{48,40},{56,48},{64,88... | collective-permute-start | bytes 1572872 | tf_op jit(solution)/shard_map/ppermute | solution.py:315
  53.4 14.1 %collective-permute-start.12 = (bf16[256,1024]{1,0:T(8,128)(2,1)}, bf16[256,1024]{1,0:T(8,128)(2,1)S(1)}, u32[]{:S(2)}, u32[]{:S(2)}) collective-permute-start(bf16[256,1024]{1,0:T(8,128)(2,1)} %get-tuple-element.85.refs_1_), channel_id=1, source_target_pairs={{0,8},{8,16},{16,24},{24,0},{32,40},{40,48},{48,56},{56,32},{64,72... | collective-permute-start | bytes 1572872 | tf_op jit(solution)/shard_map/ppermute | solution.py:315
  60.8 10.0 %collective-permute-start.15 = (bf16[512,256]{1,0:T(8,128)(2,1)S(1)}, bf16[512,256]{1,0:T(8,128)(2,1)S(1)}, u32[]{:S(2)}, u32[]{:S(2)}) collective-permute-start(bf16[512,256]{1,0:T(8,128)(2,1)S(1)} %get-tuple-element.84), channel_id=1, source_target_pairs={{0,4},{1,5},{2,6},{3,7},{4,0},{5,1},{6,2},{7,3},{8,12},{9,13},{10,... | collective-permute-start | bytes 786440 | tf_op jit(solution)/shard_map/ppermute | solution.py:211
  71.7 13.2 %collective-permute-start.16 = (bf16[256,1024]{1,0:T(8,128)(2,1)}, bf16[256,1024]{1,0:T(8,128)(2,1)S(1)}, u32[]{:S(2)}, u32[]{:S(2)}) collective-permute-start(bf16[256,1024]{1,0:T(8,128)(2,1)} %get-tuple-element.85.refs_1_), channel_id=1, source_target_pairs={{0,24},{8,0},{16,8},{24,16},{32,56},{40,32},{48,40},{56,48},{64,88... | collective-permute-start | bytes 1572872 | tf_op jit(solution)/shard_map/ppermute | solution.py:315
  72.0 14.1 %collective-permute-start.17 = (bf16[256,1024]{1,0:T(8,128)(2,1)}, bf16[256,1024]{1,0:T(8,128)(2,1)S(1)}, u32[]{:S(2)}, u32[]{:S(2)}) collective-permute-start(bf16[256,1024]{1,0:T(8,128)(2,1)} %get-tuple-element.86.refs_0_), channel_id=1, source_target_pairs={{0,8},{8,16},{16,24},{24,0},{32,40},{40,48},{48,56},{56,32},{64,72... | collective-permute-start | bytes 1572872 | tf_op jit(solution)/shard_map/ppermute | solution.py:315
  91.3 13.0 %collective-permute-start.25 = (bf16[256,1024]{1,0:T(8,128)(2,1)S(1)}, bf16[256,1024]{1,0:T(8,128)(2,1)S(1)}, u32[]{:S(2)}, u32[]{:S(2)}) collective-permute-start(bf16[256,1024]{1,0:T(8,128)(2,1)S(1)} %collective-permute-done.11.refs_0_), channel_id=1, source_target_pairs={{0,24},{8,0},{16,8},{24,16},{32,56},{40,32},{48,40},{56,48},{64,88... | collective-permute-start | bytes 1572872 | tf_op jit(solution)/shard_map/ppermute | solution.py:315
  92.7 13.9 %collective-permute-start.26 = (bf16[256,1024]{1,0:T(8,128)(2,1)S(1)}, bf16[256,1024]{1,0:T(8,128)(2,1)S(1)}, u32[]{:S(2)}, u32[]{:S(2)}) collective-permute-start(bf16[256,1024]{1,0:T(8,128)(2,1)S(1)} %collective-permute-done.12.refs_1_), channel_id=1, source_target_pairs={{0,8},{8,16},{16,24},{24,0},{32,40},{40,48},{48,56},{56,32},{64,72... | collective-permute-start | bytes 1572872 | tf_op jit(solution)/shard_map/ppermute | solution.py:315
  106.6 12.0 %collective-permute-start.28 = (bf16[256,1024]{1,0:T(8,128)(2,1)S(1)}, bf16[256,1024]{1,0:T(8,128)(2,1)S(1)}, u32[]{:S(2)}, u32[]{:S(2)}) collective-permute-start(bf16[256,1024]{1,0:T(8,128)(2,1)S(1)} %collective-permute-done.25.refs_0_), channel_id=1, source_target_pairs={{0,1},{1,0},{2,3},{3,2},{4,5},{5,4},{6,7},{7,6},{8,9},{9,8},{10,11... | collective-permute-start | bytes 1572872 | tf_op jit(solution)/shard_map/ppermute | solution.py:312
  108.3 10.3 %collective-permute-start.29 = (bf16[256,1024]{1,0:T(8,128)(2,1)S(1)}, bf16[256,1024]{1,0:T(8,128)(2,1)S(1)}, u32[]{:S(2)}, u32[]{:S(2)}) collective-permute-start(bf16[256,1024]{1,0:T(8,128)(2,1)S(1)} %collective-permute-done.26.refs_1_), channel_id=1, source_target_pairs={{0,1},{1,0},{2,3},{3,2},{4,5},{5,4},{6,7},{7,6},{8,9},{9,8},{10,11... | collective-permute-start | bytes 1572872 | tf_op jit(solution)/shard_map/ppermute | solution.py:312
  109.8 16.4 %collective-permute-start.31 = (bf16[512,256]{1,0:T(8,128)(2,1)S(1)}, bf16[512,256]{1,0:T(8,128)(2,1)S(1)}, u32[]{:S(2)}, u32[]{:S(2)}) collective-permute-start(bf16[512,256]{1,0:T(8,128)(2,1)S(1)} %get-tuple-element.108), channel_id=1, source_target_pairs={{0,2},{1,3},{2,4},{3,5},{4,6},{5,7},{6,0},{7,1},{8,10},{9,11},{10,... | collective-permute-start | bytes 786440 | tf_op jit(solution)/shard_map/ppermute | solution.py:211
  109.8 18.5 %collective-permute-start.32 = (bf16[512,256]{1,0:T(8,128)(2,1)}, bf16[512,256]{1,0:T(8,128)(2,1)S(1)}, u32[]{:S(2)}, u32[]{:S(2)}) collective-permute-start(bf16[512,256]{1,0:T(8,128)(2,1)} %get-tuple-element.109), channel_id=1, source_target_pairs={{0,4},{1,5},{2,6},{3,7},{4,0},{5,1},{6,2},{7,3},{8,12},{9,13},{10,... | collective-permute-start | bytes 786440 | tf_op jit(solution)/shard_map/ppermute | solution.py:211
  115.7 12.6 %collective-permute-start.33 = (bf16[512,256]{1,0:T(8,128)(2,1)}, bf16[512,256]{1,0:T(8,128)(2,1)S(1)}, u32[]{:S(2)}, u32[]{:S(2)}) collective-permute-start(bf16[512,256]{1,0:T(8,128)(2,1)} %get-tuple-element.110), channel_id=1, source_target_pairs={{0,6},{1,7},{2,0},{3,1},{4,2},{5,3},{6,4},{7,5},{8,14},{9,15},{10,... | collective-permute-start | bytes 786440 | tf_op jit(solution)/shard_map/ppermute | solution.py:211
  124.9 9.2 %collective-permute-start.35 = (bf16[512,256]{1,0:T(8,128)(2,1)S(1)}, bf16[512,256]{1,0:T(8,128)(2,1)S(1)}, u32[]{:S(2)}, u32[]{:S(2)}) collective-permute-start(bf16[512,256]{1,0:T(8,128)(2,1)S(1)} %get-tuple-element.113), channel_id=1, source_target_pairs={{0,4},{1,5},{2,6},{3,7},{4,0},{5,1},{6,2},{7,3},{8,12},{9,13},{10,... | collective-permute-start | bytes 786440 | tf_op jit(solution)/shard_map/ppermute | solution.py:211
  138.7 16.1 %all-to-all-start = ((bf16[16,4,32,256]{3,2,1,0:T(8,128)(2,1)}), bf16[16,4,32,256]{3,2,1,0:T(8,128)(2,1)S(1)}, u32[]{:S(2)}, u32[]{:S(2)}) async-start(bf16[16,4,32,256]{3,2,1,0:T(8,128)(2,1)} %shard_map.69), calls=%async_computation | async-start | bytes 2097152 | tf_op jit(solution)/shard_map/all_to_all | solution.py:338
  154.8 11.0 %collective-permute-start.37 = (bf16[4,2,4,32,256]{4,3,2,1,0:T(8,128)(2,1)S(1)}, bf16[4,2,4,32,256]{4,3,2,1,0:T(8,128)(2,1)S(1)}, u32[]{:S(2)}, u32[]{:S(2)}) collective-permute-start(bf16[4,2,4,32,256]{4,3,2,1,0:T(8,128)(2,1)S(1)} %dynamic-slice_bitcast_fusion), channel_id=1, source_target_pairs={{0,1},{1,0},{2,3},{3,2},{4,5},{5,4},{6,7},{7,6},{8,9},{9,8},{10,11... | collective-permute-start | bytes 1572872 | tf_op jit(solution)/shard_map/ppermute | solution.py:312
  (31 other events, 307.1 us)
